TPU v7x, 128 devices: a whole 4x4x4 slice. The times are simulated.
128 devices in a mesh: seq: 2 (over z_hi), head: 2 (over z_lo), blk: 32 (over y, x, core).
Axes of the slice: x: 4, y: 4, z: 4 (z_hi: 2, z_lo: 2; z = z_hi * 2 + z_lo), core: 2. Of those that a mesh axis runs over, the one named last changes fastest.
Arguments:
- inputs: bfloat16 [2, 8192, 1024], P('seq', ('blk', 'head')), may hold values from -6 to 6
- w_query: bfloat16 [1024, 2048], P(('seq', 'head', 'blk')), may hold values from -0.1875 to 0.1875
- key_weight: bfloat16 [1024, 1024], P(('seq', 'head', 'blk')), may hold values from -0.1875 to 0.1875
- value_weight: bfloat16 [1024, 1024], P(('seq', 'head', 'blk')), may hold values from -0.1875 to 0.1875
- w_output: bfloat16 [2048, 1024], P(('seq', 'head', 'blk')), may hold values from -6 to 6
- w_gate: bfloat16 [1024, 3072], P(('seq', 'head', 'blk')), may hold values from -0.1875 to 0.1875
- w_up: bfloat16 [1024, 3072], P(('seq', 'head', 'blk')), may hold values from -0.1875 to 0.1875
- w_down: bfloat16 [3072, 1024], P(('seq', 'head', 'blk')), may hold values from -0.109375 to 0.109375
- gain_attn: float32 [1024], replicated, may hold values from 0.5 to 1.5
- gain_ffn: float32 [1024], replicated, may hold values from 0.5 to 1.5
- gain_query: float32 [128], replicated, may hold values from 0.5 to 1.5
- gain_key: float32 [128], replicated, may hold values from 0.5 to 1.5
- grad_outputs: bfloat16 [2, 8192, 1024], P('seq', ('blk', 'head')), may hold values from -6 to 6
Outputs:
- result: bfloat16 [2, 8192, 1024], P('seq', ('blk', 'head'))
- grad_inputs: bfloat16 [2, 8192, 1024], P('seq', ('blk', 'head'))
- grad_w_query: float32 [1024, 2048], P(('seq', 'head', 'blk'))
- grad_w_key: float32 [1024, 1024], P(('seq', 'head', 'blk'))
- grad_w_value: float32 [1024, 1024], P(('seq', 'head', 'blk'))
- grad_w_output: float32 [2048, 1024], P(('seq', 'head', 'blk'))
- grad_w_gate: float32 [1024, 3072], P(('seq', 'head', 'blk'))
- grad_w_up: float32 [1024, 3072], P(('seq', 'head', 'blk'))
- grad_w_down: float32 [3072, 1024], P(('seq', 'head', 'blk'))
- grad_gain_attn: float32 [1024], replicated
- grad_gain_ffn: float32 [1024], replicated
- grad_gain_query: float32 [128], replicated
- grad_gain_key: float32 [128], replicated
All inputs are finite; a program needn't handle non-finite values.
Results may differ from a plain program's by a relative error of at most 0.024.
Values may be sent and summed in bfloat16 or wider, within the bound.
No kernel may reach another device: no remote copies, remote signals or barrier semaphores. Data moves between devices by JAX's collectives and lax.ppermute only.
A program may use at most 256 MiB of HBM per device.

v0:
```python
import jax
import jax.numpy as jnp
from jax import lax
from jax.sharding import PartitionSpec as P

epsilon = 1e-06
rope_base = 1000000.0
masked_value = -1e30


def rms_scale(values, gain):
    return values * lax.rsqrt(jnp.mean(values * values, axis=-1, keepdims=True) + epsilon) * gain


def rotate(values, cosine, sine):
    half = values.shape[-1] // 2
    first = values[..., :half]
    second_result = values[..., half:]
    return jnp.concatenate(
        [first * cosine - second_result * sine, second_result * cosine + first * sine], axis=-1
    )


def rope_tables(positions, width):
    freqs = rope_base ** (-(jnp.arange(width // 2, dtype=jnp.float32) * 2.0 / width))
    angles = positions.astype(jnp.float32)[:, None] * freqs[None, :]
    return (jnp.cos(angles)[:, None, :], jnp.sin(angles)[:, None, :])


def head_shape(raw, gain, cosine, sine, factor):
    return rotate(rms_scale(raw, gain), cosine, sine) * factor


def causal_mask(query_start, rows, key_start, width):
    query_pos = query_start + jnp.arange(rows, dtype=jnp.int32)
    key_pos = key_start + jnp.arange(width, dtype=jnp.int32)
    return (key_pos[None, :] <= query_pos[:, None])[:, None, None, :]


def score_block(carry, query, key_blk, value_blk, key_start, query_start):
    best, total, accum = carry
    scores = jnp.einsum("qhgd,khd->qhgk", query, key_blk, preferred_element_type=jnp.float32)
    allowed = causal_mask(query_start, query.shape[0], key_start, key_blk.shape[0])
    scores = jnp.where(allowed, scores, masked_value)
    fresh = jnp.maximum(best, jnp.max(scores, axis=-1))
    decay = jnp.exp(best - fresh)
    weights = jnp.where(allowed, jnp.exp(scores - fresh[..., None]), 0.0)
    total = total * decay + jnp.sum(weights, axis=-1)
    accum = accum * decay[..., None] + jnp.einsum(
        "qhgk,khd->qhgd",
        weights.astype(jnp.bfloat16),
        value_blk,
        preferred_element_type=jnp.float32,
    )
    return (fresh, total, accum)


def sweep_keys(carry, query, key_part, value_part, query_start):
    width = key_part.shape[0]
    block = 512
    last_row = query_start + query.shape[0] - 1

    def sweep_step(state, index):
        begin = index * block
        key_blk = lax.dynamic_slice_in_dim(key_part, index * block, block, 0)
        value_blk = lax.dynamic_slice_in_dim(value_part, index * block, block, 0)
        state = lax.cond(
            begin <= last_row,
            lambda inner: score_block(inner, query, key_blk, value_blk, begin, query_start),
            lambda inner: inner,
            state,
        )
        return (state, None)

    carry, _ = lax.scan(sweep_step, carry, jnp.arange(width // block, dtype=jnp.int32))
    return carry


def attention_back(query, grad_out, key_all, value_all, logsum, delta, query_start):
    length = key_all.shape[0]
    block = 512
    last_row = query_start + query.shape[0] - 1
    start_state = (
        jnp.zeros(query.shape, jnp.float32),
        jnp.zeros(key_all.shape, jnp.float32),
        jnp.zeros(value_all.shape, jnp.float32),
    )

    def work(begin, state):
        grad_query, grad_key, grad_value = state
        key_blk = lax.dynamic_slice_in_dim(key_all, begin, block, 0)
        value_blk = lax.dynamic_slice_in_dim(value_all, begin, block, 0)
        scores = jnp.einsum("qhgd,khd->qhgk", query, key_blk, preferred_element_type=jnp.float32)
        allowed = causal_mask(query_start, query.shape[0], begin, block)
        probs = jnp.where(allowed, jnp.exp(scores - logsum[..., None]), 0.0)
        grad_probs = jnp.einsum(
            "qhgd,khd->qhgk", grad_out, value_blk, preferred_element_type=jnp.float32
        )
        grad_scores = (probs * (grad_probs - delta[..., None])).astype(jnp.bfloat16)
        grad_query = grad_query + jnp.einsum(
            "qhgk,khd->qhgd", grad_scores, key_blk, preferred_element_type=jnp.float32
        )
        key_term = jnp.einsum(
            "qhgk,qhgd->khd", grad_scores, query, preferred_element_type=jnp.float32
        )
        value_term = jnp.einsum(
            "qhgk,qhgd->khd",
            probs.astype(jnp.bfloat16),
            grad_out,
            preferred_element_type=jnp.float32,
        )
        grad_key = lax.dynamic_update_slice_in_dim(grad_key, key_term, begin, 0)
        grad_value = lax.dynamic_update_slice_in_dim(grad_value, value_term, begin, 0)
        return (grad_query, grad_key, grad_value)

    def attention_step(state, index):
        begin = index * block
        state = lax.cond(
            begin <= last_row, lambda inner: work(begin, inner), lambda inner: inner, state
        )
        return (state, None)

    state, _ = lax.scan(attention_step, start_state, jnp.arange(length // block, dtype=jnp.int32))
    return state


def local(
    inputs,
    w_query,
    key_weight,
    value_weight,
    w_output,
    w_gate,
    w_up,
    w_down,
    gain_attn,
    gain_ffn,
    gain_query,
    gain_key,
    grad_outputs,
):
    w_query_all, w_key_all, w_value_all, w_output_all = (
        lax.all_gather(w_query, ("seq", "head", "blk"), axis=0, tiled=True),
        lax.all_gather(key_weight, ("seq", "head", "blk"), axis=0, tiled=True),
        lax.all_gather(value_weight, ("seq", "head", "blk"), axis=0, tiled=True),
        lax.all_gather(w_output, ("seq", "head", "blk"), axis=0, tiled=True),
    )
    w_gate_all, w_up_all, w_down_all = (
        lax.all_gather(w_gate, ("seq", "head", "blk"), axis=0, tiled=True),
        lax.all_gather(w_up, ("seq", "head", "blk"), axis=0, tiled=True),
        lax.all_gather(w_down, ("seq", "head", "blk"), axis=0, tiled=True),
    )
    tokens = inputs[0].astype(jnp.float32)
    count = tokens.shape[0]
    head_dim = gain_query.shape[0]
    factor = head_dim ** (-0.5)
    first_pos = (lax.axis_index("blk") * lax.axis_size("head") + lax.axis_index("head")) * count
    cosine, sine = rope_tables(first_pos + jnp.arange(count, dtype=jnp.int32), head_dim)
    hidden_one = rms_scale(tokens, gain_attn).astype(jnp.bfloat16)
    q_raw = jnp.dot(hidden_one, w_query_all, preferred_element_type=jnp.float32).reshape(
        count, -1, head_dim
    )
    k_raw = jnp.dot(hidden_one, w_key_all, preferred_element_type=jnp.float32).reshape(
        count, -1, head_dim
    )
    value_loc = (
        jnp.dot(hidden_one, w_value_all, preferred_element_type=jnp.float32)
        .astype(jnp.bfloat16)
        .reshape(count, -1, head_dim)
    )
    query_loc = head_shape(q_raw, gain_query, cosine, sine, factor).astype(jnp.bfloat16)
    key_loc = head_shape(k_raw, gain_key, cosine, sine, 1.0).astype(jnp.bfloat16)
    query_x, key_x, value_x = (
        lax.all_to_all(query_loc, "head", split_axis=1, concat_axis=0, tiled=True),
        lax.all_to_all(key_loc, "head", split_axis=1, concat_axis=0, tiled=True),
        lax.all_to_all(value_loc, "head", split_axis=1, concat_axis=0, tiled=True),
    )
    rows = query_x.shape[0]
    kv_heads = key_x.shape[1]
    groups = query_x.shape[1] // kv_heads
    query_grouped = query_x.reshape(rows, kv_heads, groups, head_dim)
    query_start = lax.axis_index("blk") * rows
    start_carry = (
        jnp.full((rows, kv_heads, groups), masked_value, jnp.float32),
        jnp.zeros((rows, kv_heads, groups), jnp.float32),
        jnp.zeros((rows, kv_heads, groups, head_dim), jnp.float32),
    )
    best, total, accum = sweep_keys(
        start_carry,
        query_grouped,
        lax.all_gather(key_x, "blk", axis=0, tiled=True),
        lax.all_gather(value_x, "blk", axis=0, tiled=True),
        query_start,
    )
    attended = accum / total[..., None]
    logsum = best + jnp.log(total)
    attended_send = attended.astype(jnp.bfloat16).reshape(rows, kv_heads * groups, head_dim)
    attended_loc = lax.all_to_all(
        attended_send, "head", split_axis=0, concat_axis=1, tiled=True
    ).reshape(count, -1)
    mid = tokens + jnp.dot(attended_loc, w_output_all, preferred_element_type=jnp.float32)
    hidden_after_attention = rms_scale(mid, gain_ffn).astype(jnp.bfloat16)
    gate = jnp.dot(hidden_after_attention, w_gate_all, preferred_element_type=jnp.float32)
    up_proj = jnp.dot(hidden_after_attention, w_up_all, preferred_element_type=jnp.float32)
    act = (jax.nn.silu(gate) * up_proj).astype(jnp.bfloat16)
    result = (mid + jnp.dot(act, w_down_all, preferred_element_type=jnp.float32)).astype(
        jnp.bfloat16
    )
    w_query_all, w_key_all, w_value_all, w_output_all, w_gate_all, w_up_all, w_down_all = (
        lax.all_gather(w_query, ("seq", "head", "blk"), axis=0, tiled=True),
        lax.all_gather(key_weight, ("seq", "head", "blk"), axis=0, tiled=True),
        lax.all_gather(value_weight, ("seq", "head", "blk"), axis=0, tiled=True),
        lax.all_gather(w_output, ("seq", "head", "blk"), axis=0, tiled=True),
        lax.all_gather(w_gate, ("seq", "head", "blk"), axis=0, tiled=True),
        lax.all_gather(w_up, ("seq", "head", "blk"), axis=0, tiled=True),
        lax.all_gather(w_down, ("seq", "head", "blk"), axis=0, tiled=True),
    )
    grad_rows = grad_outputs[0]
    grad_w_down = jnp.einsum("tf,td->fd", act, grad_rows, preferred_element_type=jnp.float32)
    grad_act = jnp.einsum("td,fd->tf", grad_rows, w_down_all, preferred_element_type=jnp.float32)
    _, pull_gate = jax.vjp(lambda left, right: jax.nn.silu(left) * right, gate, up_proj)
    grad_gate, grad_up = pull_gate(grad_act)
    grad_gate = grad_gate.astype(jnp.bfloat16)
    grad_up = grad_up.astype(jnp.bfloat16)
    grad_w_gate = jnp.einsum(
        "td,tf->df", hidden_after_attention, grad_gate, preferred_element_type=jnp.float32
    )
    grad_w_up = jnp.einsum(
        "td,tf->df", hidden_after_attention, grad_up, preferred_element_type=jnp.float32
    )
    grad_hidden_two = jnp.einsum(
        "tf,df->td", grad_gate, w_gate_all, preferred_element_type=jnp.float32
    ) + jnp.einsum("tf,df->td", grad_up, w_up_all, preferred_element_type=jnp.float32)
    _, pull_two = jax.vjp(rms_scale, mid, gain_ffn)
    grad_mid_norm, grad_gain_ffn = pull_two(grad_hidden_two)
    grad_mid = grad_rows.astype(jnp.float32) + grad_mid_norm
    grad_mid_low = grad_mid.astype(jnp.bfloat16)
    grad_w_output = jnp.einsum(
        "te,td->ed", attended_loc, grad_mid_low, preferred_element_type=jnp.float32
    )
    grad_attended = (
        jnp.einsum("td,ed->te", grad_mid_low, w_output_all, preferred_element_type=jnp.float32)
        .astype(jnp.bfloat16)
        .reshape(count, -1, head_dim)
    )
    grad_att_x = lax.all_to_all(
        grad_attended, "head", split_axis=1, concat_axis=0, tiled=True
    ).reshape(rows, kv_heads, groups, head_dim)
    delta = jnp.sum(grad_att_x.astype(jnp.float32) * attended, axis=-1)
    key_all, value_all = (
        lax.all_gather(key_x, "blk", axis=0, tiled=True),
        lax.all_gather(value_x, "blk", axis=0, tiled=True),
    )
    grad_query_g, grad_key_all, grad_value_all = attention_back(
        query_grouped, grad_att_x, key_all, value_all, logsum, delta, query_start
    )
    grad_key_x, grad_value_x = (
        lax.psum_scatter(
            grad_key_all.astype(jnp.bfloat16), "blk", scatter_dimension=0, tiled=True
        ).astype(jnp.float32),
        lax.psum_scatter(
            grad_value_all.astype(jnp.bfloat16), "blk", scatter_dimension=0, tiled=True
        ).astype(jnp.float32),
    )
    grad_query_x = grad_query_g.astype(jnp.bfloat16).reshape(rows, kv_heads * groups, head_dim)
    grad_q_loc, grad_k_loc, grad_v_loc = (
        lax.all_to_all(grad_query_x, "head", split_axis=0, concat_axis=1, tiled=True),
        lax.all_to_all(
            grad_key_x.astype(jnp.bfloat16), "head", split_axis=0, concat_axis=1, tiled=True
        ),
        lax.all_to_all(
            grad_value_x.astype(jnp.bfloat16), "head", split_axis=0, concat_axis=1, tiled=True
        ),
    )
    _, pull_query = jax.vjp(
        lambda raw, gain: head_shape(raw, gain, cosine, sine, factor), q_raw, gain_query
    )
    grad_q_raw, grad_gain_query = pull_query(grad_q_loc.astype(jnp.float32))
    _, pull_key = jax.vjp(
        lambda raw, gain: head_shape(raw, gain, cosine, sine, 1.0), k_raw, gain_key
    )
    grad_k_raw, grad_gain_key = pull_key(grad_k_loc.astype(jnp.float32))
    grad_q_low = grad_q_raw.reshape(count, -1).astype(jnp.bfloat16)
    grad_k_low = grad_k_raw.reshape(count, -1).astype(jnp.bfloat16)
    grad_v_low = grad_v_loc.reshape(count, -1)
    grad_w_query = jnp.einsum(
        "td,te->de", hidden_one, grad_q_low, preferred_element_type=jnp.float32
    )
    grad_w_key = jnp.einsum("td,te->de", hidden_one, grad_k_low, preferred_element_type=jnp.float32)
    grad_w_value = jnp.einsum(
        "td,te->de", hidden_one, grad_v_low, preferred_element_type=jnp.float32
    )
    grad_hidden_one = jnp.einsum(
        "te,de->td", grad_q_low, w_query_all, preferred_element_type=jnp.float32
    )
    grad_hidden_one = grad_hidden_one + jnp.einsum(
        "te,de->td", grad_k_low, w_key_all, preferred_element_type=jnp.float32
    )
    grad_hidden_one = grad_hidden_one + jnp.einsum(
        "te,de->td", grad_v_low, w_value_all, preferred_element_type=jnp.float32
    )
    _, pull_one = jax.vjp(rms_scale, tokens, gain_attn)
    grad_tok_norm, grad_gain_attn = pull_one(grad_hidden_one)
    grad_inputs = (grad_mid + grad_tok_norm).astype(jnp.bfloat16)
    shard_query, shard_key, value_shard_piece, shard_output = (
        lax.psum_scatter(grad_w_query, ("seq", "head", "blk"), scatter_dimension=0, tiled=True),
        lax.psum_scatter(grad_w_key, ("seq", "head", "blk"), scatter_dimension=0, tiled=True),
        lax.psum_scatter(grad_w_value, ("seq", "head", "blk"), scatter_dimension=0, tiled=True),
        lax.psum_scatter(grad_w_output, ("seq", "head", "blk"), scatter_dimension=0, tiled=True),
    )
    shard_gate, shard_up, shard_down = (
        lax.psum_scatter(grad_w_gate, ("seq", "head", "blk"), scatter_dimension=0, tiled=True),
        lax.psum_scatter(grad_w_up, ("seq", "head", "blk"), scatter_dimension=0, tiled=True),
        lax.psum_scatter(grad_w_down, ("seq", "head", "blk"), scatter_dimension=0, tiled=True),
    )
    sum_attn, sum_ffn, sum_query, sum_key = lax.psum(
        (grad_gain_attn, grad_gain_ffn, grad_gain_query, grad_gain_key), ("seq", "head", "blk")
    )
    return (
        result[None],
        grad_inputs[None],
        shard_query,
        shard_key,
        value_shard_piece,
        shard_output,
        shard_gate,
        shard_up,
        shard_down,
        sum_attn,
        sum_ffn,
        sum_query,
        sum_key,
    )


def solution(mesh):
    in_specs = (
        P("seq", ("blk", "head"), None),
        P(("seq", "head", "blk"), None),
        P(("seq", "head", "blk"), None),
        P(("seq", "head", "blk"), None),
        P(("seq", "head", "blk"), None),
        P(("seq", "head", "blk"), None),
        P(("seq", "head", "blk"), None),
        P(("seq", "head", "blk"), None),
        P(),
        P(),
        P(),
        P(),
        P("seq", ("blk", "head"), None),
    )
    out_specs = (
        P("seq", ("blk", "head"), None),
        P("seq", ("blk", "head"), None),
        P(("seq", "head", "blk"), None),
        P(("seq", "head", "blk"), None),
        P(("seq", "head", "blk"), None),
        P(("seq", "head", "blk"), None),
        P(("seq", "head", "blk"), None),
        P(("seq", "head", "blk"), None),
        P(("seq", "head", "blk"), None),
        P(),
        P(),
        P(),
        P(),
    )
    return jax.shard_map(local, mesh=mesh, in_specs=in_specs, out_specs=out_specs, check_vma=False)
```

profile of v0, /device:TPU:0, one launch (start us, length us, event | category | flops | bytes accessed | tf_op | source)
XLA Modules:
  0.0 4464.1 jit_solution(11430290591911243942)
XLA Ops:
  11.1 67.8 %all-gather.16.cloned.1.call-done = bf16[1024,1024]{1,0:T(8,128)(2,1)} async-done(((bf16[8,1024]{1,0:T(8,128)(2,1)}), bf16[1024,1024]{1,0:T(8,128)(2,1)}) %all-gather.16.cloned.1.call-update) | async-done | bytes 2097168 | tf_op jit(solution)/shard_map/all_gather | solution.py:145
  78.9 2.2 fusion.56
  81.2 8.3 all_to_all.114
  90.5 54.3 %all-gather.10.cloned.1.call-done = bf16[1024,1024]{1,0:T(8,128)(2,1)} async-done(((bf16[8,1024]{1,0:T(8,128)(2,1)}), bf16[1024,1024]{1,0:T(8,128)(2,1)}) %all-gather.10.cloned.1.call-update) | async-done | bytes 2097168 | tf_op jit(solution)/shard_map/all_gather | solution.py:144
  144.8 3.9 copy.90
  148.8 2.4 multiply_reduce_fusion.9
  152.2 8.4 all_to_all.115
  164.3 48.1 %all-gather.14.cloned.1.call-done = bf16[1024,2048]{1,0:T(8,128)(2,1)} async-done(((bf16[8,2048]{1,0:T(8,128)(2,1)}), bf16[1024,2048]{1,0:T(8,128)(2,1)}) %all-gather.14.cloned.1.call-update) | async-done | bytes 4194320 | tf_op jit(solution)/shard_map/all_gather | solution.py:143
  212.4 6.4 copy.92
  218.8 3.6 multiply_reduce_fusion.3
  224.7 3.5 all-to-all-start.1
  228.2 8.7 all-to-all-done.1
  237.1 28.3 all-gather.18.cloned.1.call-done
  265.4 55.2 %all-gather.12.cloned.1.call-done = bf16[8192,4,128]{2,0,1:T(8,128)(2,1)} async-done(((bf16[256,4,128]{2,0,1:T(8,128)(2,1)}), bf16[8192,4,128]{2,0,1:T(8,128)(2,1)}) %all-gather.12.cloned.1.call-update) | async-done | bytes 8388624 | tf_op jit(solution)/shard_map/all_gather | solution.py:191
  320.8 26.2 while.28
  322.0 5.7 conditional.4
  322.2 1.8 fusion
  324.9 2.8 fusion.12
  347.9 12.3 all_to_all.116
  360.6 29.6 all-gather.20.cloned.1.call-done
  390.2 3.0 multiply_reduce_fusion.8
  393.4 65.8 %all-gather.24.cloned.1.call-done = bf16[1024,3072]{1,0:T(8,128)(2,1)} async-done(((bf16[8,3072]{1,0:T(8,128)(2,1)}), bf16[1024,3072]{1,0:T(8,128)(2,1)}) %all-gather.24.cloned.1.call-update) | async-done | bytes 6291472 | tf_op jit(solution)/shard_map/all_gather | solution.py:150
  459.2 5.0 fusion.108
  464.1 64.0 %all-gather.22.cloned.1.call-done = bf16[1024,3072]{1,0:T(8,128)(2,1)} async-done(((bf16[8,3072]{1,0:T(8,128)(2,1)}), bf16[1024,3072]{1,0:T(8,128)(2,1)}) %all-gather.22.cloned.1.call-update) | async-done | bytes 6291472 | tf_op jit(solution)/shard_map/all_gather | solution.py:149
  528.2 4.9 fusion.107
  533.1 64.1 %all-gather.26.cloned.1.call-done = bf16[3072,1024]{1,0:T(8,128)(2,1)} async-done(((bf16[24,1024]{1,0:T(8,128)(2,1)}), bf16[3072,1024]{1,0:T(8,128)(2,1)}) %all-gather.26.cloned.1.call-update) | async-done | bytes 6291472 | tf_op jit(solution)/shard_map/all_gather | solution.py:151
  597.1 7.3 multiply_convert_fusion
  604.5 2.2 fusion.109
  606.7 5.3 multiply_reduce_fusion.5
  614.7 3.5 all-to-all-start.4
  618.2 8.6 all-to-all-done.4
  629.5 4.3 broadcast.300.clone
  633.8 4.4 broadcast.300
  638.2 40.6 while.29
  639.6 19.9 conditional.5
  639.8 1.8 fusion.38
  641.6 2.5 fusion.25
  644.1 1.7 fusion.37
  645.8 1.8 fusion.34
  648.4 5.6 dynamic_update_slice.4
  654.0 5.6 dynamic_update_slice.5
  678.8 12.3 copy.142
  691.1 40.0 copy.143
  732.3 4.5 fusion.95
  737.7 7.5 fusion.79
  746.2 7.5 fusion.113
  753.7 7.6 fusion.112
  763.2 441.3 %all-reduce.10.cloned.1.call-done = (bf16[8192,4,128]{2,1,0:T(4,128)(2,1)}, bf16[8192,4,128]{2,1,0:T(4,128)(2,1)}) async-done(((bf16[8192,4,128]{2,1,0:T(4,128)(2,1)}, bf16[8192,4,128]{2,1,0:T(4,128)(2,1)}), (bf16[8192,4,128]{2,1,0:T(4,128)(2,1)}, bf16[8192,4,128]{2,1,0:T(4,128)(2,1)})) %all-reduce.10.cloned.1.call-update) | async-done | bytes 16777232
  1205.6 7.8 all_to_all.117
  1216.6 2.8 fusion.91
  1220.5 7.6 all_to_all.118
  1228.3 2.8 fusion.89
  1232.5 10.3 all_to_all.119
  1243.9 2.5 copy.102
  1249.3 4.7 fusion.87
  1255.1 4.7 fusion.57
  1263.8 68.1 %all-reduce.6 = (f32[1024]{0:T(1024)}, f32[1024]{0:T(1024)}, f32[128]{0:T(128)}, f32[128]{0:T(128)}) all-reduce(f32[1024]{0:T(1024)S(1)} %get-tuple-element.347, f32[1024]{0:T(1024)S(1)} %get-tuple-element.345, f32[128]{0:T(128)S(1)} %get-tuple-element.341, ...), channel_id=1, replica_groups=mesh['seq'=2,'head'=2,'blk'=32] {'seq','head','blk'}, use_global_device_ids=true, to_apply=%region_29.30 | all-reduce | flops 2304 | bytes 18432 | tf_op jit(solution)/shard_map/psum | solution.py:316
  1332.8 525.4 %reduce-scatter.14.cloned.1.call-done = f32[16,1024]{1,0:T(8,128)} async-done(((f32[2048,1024]{1,0:T(8,128)}), f32[16,1024]{1,0:T(8,128)}) %reduce-scatter.14.cloned.1.call-update) | async-done | bytes 65552 | tf_op jit(solution)/shard_map/reduce_scatter | solution.py:309
  1858.2 220.7 %reduce-scatter.20.cloned.1.call-done = f32[24,1024]{1,0:T(8,128)} async-done(((f32[3072,1024]{1,0:T(8,128)}), f32[24,1024]{1,0:T(8,128)}) %reduce-scatter.20.cloned.1.call-update) | async-done | bytes 98320 | tf_op jit(solution)/shard_map/reduce_scatter | solution.py:314
  2079.0 224.7 %reduce-scatter.18.cloned.1.call-done = f32[8,3072]{1,0:T(8,128)} async-done(((f32[1024,3072]{1,0:T(8,128)}), f32[8,3072]{1,0:T(8,128)}) %reduce-scatter.18.cloned.1.call-update) | async-done | bytes 98320 | tf_op jit(solution)/shard_map/reduce_scatter | solution.py:313
  2303.7 224.6 %reduce-scatter.16.cloned.1.call-done = f32[8,3072]{1,0:T(8,128)} async-done(((f32[1024,3072]{1,0:T(8,128)}), f32[8,3072]{1,0:T(8,128)}) %reduce-scatter.16.cloned.1.call-update) | async-done | bytes 98320 | tf_op jit(solution)/shard_map/reduce_scatter | solution.py:312
  2528.3 642.9 %reduce-scatter.10.cloned.1.call-done = f32[8,1024]{1,0:T(8,128)} async-done(((f32[1024,1024]{1,0:T(8,128)}), f32[8,1024]{1,0:T(8,128)}) %reduce-scatter.10.cloned.1.call-update) | async-done | bytes 32784 | tf_op jit(solution)/shard_map/reduce_scatter | solution.py:307
  3171.3 639.2 %reduce-scatter.12.cloned.1.call-done = f32[8,1024]{1,0:T(8,128)} async-done(((f32[1024,1024]{1,0:T(8,128)}), f32[8,1024]{1,0:T(8,128)}) %reduce-scatter.12.cloned.1.call-update) | async-done | bytes 32784 | tf_op jit(solution)/shard_map/reduce_scatter | solution.py:308
  3810.4 646.7 %reduce-scatter.8.cloned.1.call-done = f32[8,2048]{1,0:T(8,128)} async-done(((f32[1024,2048]{1,0:T(8,128)}), f32[8,2048]{1,0:T(8,128)}) %reduce-scatter.8.cloned.1.call-update) | async-done | bytes 65552 | tf_op jit(solution)/shard_map/reduce_scatter | solution.py:306
  (254 shorter events, 61.0 us)
Async XLA Ops:
  7.2 71.7 %all-gather.16.cloned.1.call-start = ((), (), s32[]{:S(2)}) async-start(), calls=%async_computation.18 | async-start | bytes 2113536 | tf_op jit(solution)/shard_map/all_gather | solution.py:145
  7.9 136.9 %all-gather.10.cloned.1.call-start = ((), (), s32[]{:S(2)}) async-start(), calls=%async_computation.15 | async-start | bytes 2113536 | tf_op jit(solution)/shard_map/all_gather | solution.py:144
  8.7 203.7 %all-gather.14.cloned.1.call-start = ((), (), s32[]{:S(2)}) async-start(), calls=%async_computation.17 | async-start | bytes 4227072 | tf_op jit(solution)/shard_map/all_gather | solution.py:143
  9.4 256.0 %all-gather.18.cloned.1.call-start = ((), (), s32[]{:S(2)}) async-start(), calls=%async_computation.19 | async-start | bytes 8650752 | tf_op jit(solution)/shard_map/all_gather | solution.py:192
  10.5 0.5 copy-start.42
  11.1 137.7 %copy-start.2 = (bf16[1,128,1024]{2,1,0:T(8,128)(2,1)S(1)}, bf16[1,128,1024]{2,1,0:T(8,128)(2,1)}, u32[]{:S(2)}) copy-start(bf16[1,128,1024]{2,1,0:T(8,128)(2,1)} %param.21) | copy-start | bytes 786436
  11.1 137.7 %copy-start.28 = (f32[1024]{0:T(1024)S(1)}, f32[1024]{0:T(1024)}, u32[]{:S(2)}) copy-start(f32[1024]{0:T(1024)} %param.29) | copy-start | bytes 12292
  81.2 70.8 %copy-start.38 = (f32[128]{0:T(128)S(1)}, f32[128]{0:T(128)}, u32[]{:S(2)}) copy-start(f32[128]{0:T(128)} %param.32) | copy-start | bytes 1540
  90.2 230.5 %all-gather.12.cloned.1.call-start = ((), (), s32[]{:S(2)}) async-start(), calls=%async_computation.16 | async-start | bytes 8650752 | tf_op jit(solution)/shard_map/all_gather | solution.py:191
  151.2 0.8 copy-start.9
  151.2 67.6 %copy-start.36 = (f32[128,8]{0,1:T(8,128)}, f32[128,8]{0,1:T(8,128)S(1)}, u32[]{:S(2)}) copy-start(f32[128,8]{0,1:T(8,128)S(1)} %get-tuple-element.418) | copy-start | bytes 12292
  151.2 67.5 %copy-start.33 = (f32[128,8]{0,1:T(8,128)}, f32[128,8]{0,1:T(8,128)S(1)}, u32[]{:S(2)}) copy-start(f32[128,8]{0,1:T(8,128)S(1)} %fusion.99) | copy-start | bytes 12292
  161.5 228.7 %all-gather.20.cloned.1.call-start = ((), (), s32[]{:S(2)}) async-start(), calls=%async_computation.20 | async-start | bytes 4227072 | tf_op jit(solution)/shard_map/all_gather | solution.py:146
  162.1 297.1 %all-gather.24.cloned.1.call-start = ((), (), s32[]{:S(2)}) async-start(), calls=%async_computation.22 | async-start | bytes 6340608 | tf_op jit(solution)/shard_map/all_gather | solution.py:150
  162.8 365.4 %all-gather.22.cloned.1.call-start = ((), (), s32[]{:S(2)}) async-start(), calls=%async_computation.21 | async-start | bytes 6340608 | tf_op jit(solution)/shard_map/all_gather | solution.py:149
  163.6 433.6 %all-gather.26.cloned.1.call-start = ((), (), s32[]{:S(2)}) async-start(), calls=%async_computation.23 | async-start | bytes 6340608 | tf_op jit(solution)/shard_map/all_gather | solution.py:151
  218.8 4.5 copy-start.40
  222.3 1.0 copy-start.5
  222.3 98.3 %copy-start.31 = (f32[128,16]{0,1:T(8,128)}, f32[128,16]{0,1:T(8,128)S(1)}, u32[]{:S(2)}) copy-start(f32[128,16]{0,1:T(8,128)S(1)} %get-tuple-element.420) | copy-start | bytes 24580
  222.4 98.3 %copy-start.29 = (f32[128,16]{0,1:T(8,128)}, f32[128,16]{0,1:T(8,128)S(1)}, u32[]{:S(2)}) copy-start(f32[128,16]{0,1:T(8,128)S(1)} %fusion.98) | copy-start | bytes 24580
  224.7 12.2 all-to-all-start.1
  347.3 45.9 %copy-start.35 = (f32[1024]{0:T(1024)S(1)}, f32[1024]{0:T(1024)}, u32[]{:S(2)}) copy-start(f32[1024]{0:T(1024)} %param.30) | copy-start | bytes 12292
  360.6 32.7 copy-start.15
  393.3 134.8 %copy-start.7 = (bf16[128,1024]{1,0:T(8,128)(2,1)}, bf16[128,1024]{1,0:T(8,128)(2,1)S(1)}, u32[]{:S(2)}) copy-start(bf16[128,1024]{1,0:T(8,128)(2,1)S(1)} %multiply_convert_fusion.2) | copy-start | bytes 786436
  464.1 133.0 %copy-start.26 = (bf16[1,128,1024]{2,1,0:T(8,128)(2,1)S(1)}, bf16[1,128,1024]{2,1,0:T(8,128)(2,1)}, u32[]{:S(2)}) copy-start(bf16[1,128,1024]{2,1,0:T(8,128)(2,1)} %param.33) | copy-start | bytes 786436
  597.1 7.3 copy-start
  604.5 7.5 copy-start.20
  604.5 7.5 copy-start.21
  606.7 5.5 copy-start.3
  612.2 15.5 copy-start.11
  614.7 12.2 all-to-all-start.4
  618.2 586.4 %all-reduce.10.cloned.1.call-start = ((), (), s32[]{:S(2)}) async-start(), calls=%async_computation.31 | async-start | bytes 33554432
  678.8 12.3 copy-start.1
  731.1 1.0 copy-start.12
  731.1 1.2 copy-start.16
  731.1 1127.1 %reduce-scatter.14.cloned.1.call-start = ((), (), s32[]{:S(2)}) async-start(), calls=%async_computation.27 | async-start | bytes 8454144 | tf_op jit(solution)/shard_map/reduce_scatter | solution.py:309
  736.8 0.9 copy-start.27
  736.8 1342.2 %reduce-scatter.20.cloned.1.call-start = ((), (), s32[]{:S(2)}) async-start(), calls=%async_computation.30 | async-start | bytes 12681216 | tf_op jit(solution)/shard_map/reduce_scatter | solution.py:314
  745.2 0.9 copy-start.8
  745.2 1558.5 %reduce-scatter.18.cloned.1.call-start = ((), (), s32[]{:S(2)}) async-start(), calls=%async_computation.29 | async-start | bytes 12681216 | tf_op jit(solution)/shard_map/reduce_scatter | solution.py:313
  753.7 1774.6 %reduce-scatter.16.cloned.1.call-start = ((), (), s32[]{:S(2)}) async-start(), calls=%async_computation.28 | async-start | bytes 12681216 | tf_op jit(solution)/shard_map/reduce_scatter | solution.py:312
  761.3 0.7 copy-start.44
  761.3 454.2 %copy-start.10 = (f32[128,8,128]{0,2,1:T(8,128)S(1)}, f32[128,8,128]{0,2,1:T(8,128)}, u32[]{:S(2)}) copy-start(f32[128,8,128]{0,2,1:T(8,128)} %copy-done.9) | copy-start | bytes 1572868
  761.3 454.2 %copy-start.34 = (f32[128,8]{0,1:T(8,128)S(1)}, f32[128,8]{0,1:T(8,128)}, u32[]{:S(2)}) copy-start(f32[128,8]{0,1:T(8,128)} %copy-done.33) | copy-start | bytes 12292
  761.3 454.2 %copy-start.39 = (f32[128]{0:T(128)S(1)}, f32[128]{0:T(128)}, u32[]{:S(2)}) copy-start(f32[128]{0:T(128)} %param.32) | copy-start | bytes 1540
  761.3 454.3 %copy-start.37 = (f32[128,8]{0,1:T(8,128)S(1)}, f32[128,8]{0,1:T(8,128)}, u32[]{:S(2)}) copy-start(f32[128,8]{0,1:T(8,128)} %copy-done.36) | copy-start | bytes 12292
  761.4 2409.9 %reduce-scatter.10.cloned.1.call-start = ((), (), s32[]{:S(2)}) async-start(), calls=%async_computation.25 | async-start | bytes 4227072 | tf_op jit(solution)/shard_map/reduce_scatter | solution.py:307
  1215.9 0.7 copy-start.22
  1219.4 2591.0 %reduce-scatter.12.cloned.1.call-start = ((), (), s32[]{:S(2)}) async-start(), calls=%async_computation.26 | async-start | bytes 4227072 | tf_op jit(solution)/shard_map/reduce_scatter | solution.py:308
  1228.3 2.8 copy-start.24
  1231.2 3226.0 %reduce-scatter.8.cloned.1.call-start = ((), (), s32[]{:S(2)}) async-start(), calls=%async_computation.24 | async-start | bytes 8454144 | tf_op jit(solution)/shard_map/reduce_scatter | solution.py:306
  1231.3 16.5 copy-start.6
  1231.3 16.5 copy-start.30
  1231.3 16.5 copy-start.41
  1242.8 5.4 copy-start.32
  1248.4 0.8 copy-start.17
  1254.0 1.1 copy-start.19
  1255.1 4.7 copy-start.13
  1255.1 4.7 copy-start.25
  1255.1 5.5 copy-start.14
  1255.1 5.5 copy-start.23
  1259.8 2.2 copy-start.4
  1259.8 2.3 copy-start.18
  1260.7 71.2 %copy-start.43 = (f32[128]{0:T(128)S(1)}, f32[128]{0:T(128)}, u32[]{:S(2)}) copy-start(f32[128]{0:T(128)} %copy-done.42) | copy-start | bytes 1540
Sparse Core Ops, SparseCore 0:
  11.1 67.7 all-gather.15
  82.1 62.7 all-gather.9
  148.0 64.3 all-gather.13
  215.1 50.3 all-gather.17
  268.2 52.4 all-gather.11
  323.7 66.4 all-gather.19
  393.3 65.8 all-gather.23
  462.3 65.8 all-gather.21
  531.3 65.8 all-gather.25
  731.2 473.2 all-reduce.9
  1207.6 650.5 reduce-scatter.13
  1863.6 215.2 reduce-scatter.19
  2084.5 219.1 reduce-scatter.17
  2309.1 219.1 reduce-scatter.15
  2531.1 640.1 reduce-scatter.9
  3174.2 636.2 reduce-scatter.11
  3813.2 643.8 reduce-scatter.7
where the time goes:
time: 4480 us; the launch traced here: 4460 us
  waiting for transfers between devices  4070 us (91%)
  blocking collectives  123 us (3%)
  local copies, waits for them, and re-layouts  122 us (3%)
  matrix products  95.9 us (2%)
    reduce_scatter x1, waiting for transfers between devices, local(): lax.psum_scatter(grad_w_query, ('seq', 'head', 'blk'), scatter_dimension=...  647 us
    reduce_scatter x1, waiting for transfers between devices, local(): lax.psum_scatter(grad_w_key, ('seq', 'head', 'blk'), scatter_dimension=0,...  643 us
    reduce_scatter x1, waiting for transfers between devices, local(): lax.psum_scatter(grad_w_value, ('seq', 'head', 'blk'), scatter_dimension=...  639 us
    reduce_scatter x1, waiting for transfers between devices, local(): lax.psum_scatter(grad_w_output, ('seq', 'head', 'blk'), scatter_dimension...  525 us
    unnamed x18, waiting for transfers between devices  446 us
    reduce_scatter x1, waiting for transfers between devices, local(): lax.psum_scatter(grad_w_up, ('seq', 'head', 'blk'), scatter_dimension=0,...  225 us
    reduce_scatter x1, waiting for transfers between devices, local(): lax.psum_scatter(grad_w_gate, ('seq', 'head', 'blk'), scatter_dimension=0...  225 us
    reduce_scatter x1, waiting for transfers between devices, local(): lax.psum_scatter(grad_w_down, ('seq', 'head', 'blk'), scatter_dimension=0...  221 us
  transfers between devices with their start and end apart: 19, of which 19 were waited for; matrix products, arithmetic and copies ran while one was open for 2% of the time, Pallas kernels for 0%

commit v1 on v0

v1 whole, which is shorter than its diff:
```python
import functools

import jax
import jax.numpy as jnp
from jax import lax
from jax.experimental import pallas as pl
from jax.experimental.pallas import tpu as pltpu
from jax.sharding import Mesh, PartitionSpec as P

EPS = 1e-06
ROPE_BASE = 1000000.0
BF = jnp.bfloat16
F32 = jnp.float32
HD = 128
ALL = ("seq", "head", "y", "x", "core")
Z = ("seq", "head")
VMEM = pl.BlockSpec(memory_space=pltpu.VMEM)
SMEM = pl.BlockSpec(memory_space=pltpu.SMEM)
PARAMS = pltpu.CompilerParams(vmem_limit_bytes=48 * 1024 * 1024)


def swap(v, axis, m):
    n = 2 if axis == "core" or axis == "head" else 4
    return lax.ppermute(v, axis, [(i, i ^ m) for i in range(n)])


def pick4(parts, me):
    b0 = (me & 1) == 1
    b1 = (me & 2) == 2
    return [
        jnp.where(b1, jnp.where(b0, parts[k ^ 3], parts[k ^ 2]), jnp.where(b0, parts[k ^ 1], parts[k]))
        for k in range(4)
    ]


def gather_group(v):
    w = jnp.stack([v] + [swap(v, "y", d) for d in (1, 2, 3)])
    return jnp.stack([w, swap(w, "core", 1)], axis=1)


def scatter_group(part):
    s = part[:, 0] + swap(part[:, 1].astype(BF), "core", 1).astype(F32)
    sb = s.astype(BF)
    got = [swap(sb[d], "y", d).astype(F32) for d in (1, 3, 2)]
    return s[0] + got[0] + got[1] + got[2]


def exchange_group(v):
    w = jnp.stack([v[:, 0], swap(v[:, 1], "core", 1)], axis=1)
    r = {d: swap(w[d], "y", d) for d in (1, 3, 2)}
    return jnp.stack([w[0], r[1], r[2], r[3]])


def gather_x(v, me, axis):
    return jnp.stack(pick4([v] + [swap(v, "x", d) for d in (1, 2, 3)], me), axis=axis)


def gather_z(v, me):
    return jnp.stack(pick4([v] + [swap(v, Z, d) for d in (1, 2, 3)], me), axis=0)


def reduce_slots(parts, axis, me):
    parts = pick4(parts, me)
    total = parts[0]
    for d in (1, 3, 2):
        total = total + swap(parts[d].astype(BF), axis, d).astype(F32)
    return total


def qkv_kernel(x_ref, gain_ref, w_ref, gq_ref, gk_ref, cos_ref, sin_ref, h_ref, q_ref, kv_ref, raw_ref):
    x = x_ref[...].astype(F32)
    scale = lax.rsqrt(jnp.mean(x * x, axis=-1, keepdims=True) + EPS)
    h = (x * scale * gain_ref[...]).astype(BF)
    h_ref[...] = h
    raw = jnp.dot(h, w_ref[...], preferred_element_type=F32)
    raw_ref[...] = raw[:, : 3 * HD]
    cos = cos_ref[...]
    sin = sin_ref[...]

    def shaped(v, gain, factor):
        r = lax.rsqrt(jnp.mean(v * v, axis=-1, keepdims=True) + EPS)
        u = v * r * gain
        return ((u * cos + pltpu.roll(u, HD // 2, 1) * sin) * factor).astype(BF)

    factor = HD ** (-0.5)
    q_ref[:, :HD] = shaped(raw[:, :HD], gq_ref[...], factor)
    q_ref[:, HD:] = shaped(raw[:, HD : 2 * HD], gq_ref[...], factor)
    kv_ref[:, :HD] = shaped(raw[:, 2 * HD : 3 * HD], gk_ref[...], 1.0)
    kv_ref[:, HD:] = raw[:, 3 * HD :].astype(BF)


def qkv_project(x, gain, w, gq, gk, cos, sin):
    rows, width = x.shape
    tile = 256
    row = lambda n: pl.BlockSpec((tile, n), lambda i: (i, 0))
    whole = lambda a: pl.BlockSpec(a.shape, lambda i: (0, 0))
    return pl.pallas_call(
        qkv_kernel,
        grid=(rows // tile,),
        in_specs=[row(width), whole(gain), whole(w), whole(gq), whole(gk), row(HD), row(HD)],
        out_specs=[row(width), row(2 * HD), row(2 * HD), row(3 * HD)],
        out_shape=[
            jax.ShapeDtypeStruct((rows, width), BF),
            jax.ShapeDtypeStruct((rows, 2 * HD), BF),
            jax.ShapeDtypeStruct((rows, 2 * HD), BF),
            jax.ShapeDtypeStruct((rows, 3 * HD), F32),
        ],
        compiler_params=PARAMS,
        cost_estimate=pl.CostEstimate(flops=2 * rows * width * 512, bytes_accessed=8 << 20, transcendentals=0),
        name="qkv_project",
    )(x, gain, w, gq, gk, cos, sin)


def qkv_back_kernel(dq_ref, dkv_ref, raw_ref, gq_ref, gk_ref, cos_ref, sin_ref, out_ref, gain_ref):
    cos = cos_ref[...]
    sin = sin_ref[...]

    @pl.when(pl.program_id(0) == 0)
    def _():
        gain_ref[...] = jnp.zeros_like(gain_ref)

    def back(d, v, gain, factor):
        d = d.astype(F32) * factor
        d = d * cos + pltpu.roll(d * sin, HD // 2, 1)
        r = lax.rsqrt(jnp.mean(v * v, axis=-1, keepdims=True) + EPS)
        u = v * r
        t = d * gain
        raw = r * (t - u * jnp.mean(t * u, axis=-1, keepdims=True))
        return raw.astype(BF), jnp.sum(d * u, axis=0, keepdims=True)

    factor = HD ** (-0.5)
    a, ga = back(dq_ref[:, :HD], raw_ref[:, :HD], gq_ref[...], factor)
    b, gb = back(dq_ref[:, HD:], raw_ref[:, HD : 2 * HD], gq_ref[...], factor)
    c, gc = back(dkv_ref[:, :HD], raw_ref[:, 2 * HD :], gk_ref[...], 1.0)
    out_ref[:, :HD] = a
    out_ref[:, HD : 2 * HD] = b
    out_ref[:, 2 * HD : 3 * HD] = c
    out_ref[:, 3 * HD :] = dkv_ref[:, HD:]
    gain_ref[0:1, :] += ga + gb
    gain_ref[1:2, :] += gc


def qkv_back(dq, dkv, raw, gq, gk, cos, sin):
    rows = dq.shape[0]
    tile = 256
    row = lambda n: pl.BlockSpec((tile, n), lambda i: (i, 0))
    whole = lambda a: pl.BlockSpec(a.shape, lambda i: (0, 0))
    return pl.pallas_call(
        qkv_back_kernel,
        grid=(rows // tile,),
        in_specs=[row(2 * HD), row(2 * HD), row(3 * HD), whole(gq), whole(gk), row(HD), row(HD)],
        out_specs=[row(4 * HD), pl.BlockSpec((8, HD), lambda i: (0, 0))],
        out_shape=[jax.ShapeDtypeStruct((rows, 4 * HD), BF), jax.ShapeDtypeStruct((8, HD), F32)],
        compiler_params=PARAMS,
        name="qkv_back",
    )(dq, dkv, raw, gq, gk, cos, sin)


TILE = 256


def pair_of(i):
    t = jnp.where(i < 1, 1, jnp.where(i < 3, 2, 3))
    u = jnp.where(i < 1, 0, jnp.where(i < 3, i - 1, i - 3))
    return t, u


def spread(core, key_axis):
    shape = (TILE, TILE)
    a = lax.broadcasted_iota(jnp.int32, shape, key_axis)
    b = lax.broadcasted_iota(jnp.int32, shape, 1 - key_axis)
    flip = core * 128

    def place(i):
        j = i ^ flip
        return j + (j & 128)

    return place(a) - place(b)


def attend_kernel(first, last, deltas, meta_ref, *refs):
    n = len(deltas)
    q_ref = refs[0]
    kv_refs = refs[1 : 1 + n]
    at = 1 + n
    if not first:
        acc_in, sum_in = refs[at : at + 2]
        at += 2
    if last:
        att_ref, low_ref, sum_ref = refs[at : at + 3]
        acc_ref, mask_ref = refs[at + 3 :]
    else:
        acc_ref, sum_ref = refs[at : at + 2]
        (mask_ref,) = refs[at + 2 :]
    if first:
        acc_ref[...] = jnp.zeros_like(acc_ref)
        sum_ref[...] = jnp.zeros_like(sum_ref)
    else:
        acc_ref[...] = acc_in[...]
        sum_ref[...] = sum_in[...]
    y, core, x, head = meta_ref[0], meta_ref[1], meta_ref[2], meta_ref[3]
    mask_ref[...] = spread(core, 1)

    def unit(kv_ref, t, u, limit):
        rows = pl.ds(pl.multiple_of((t ^ y) * TILE, TILE), TILE)
        cols = pl.ds(pl.multiple_of((u ^ y) * TILE, TILE), TILE)
        key = kv_ref[cols, :HD]
        value = kv_ref[cols, HD:]
        for h in range(2):
            lanes = slice(h * HD, (h + 1) * HD)
            s = lax.dot_general(q_ref[rows, lanes], key, (((1,), (1,)), ((), ())), preferred_element_type=F32)
            p = jnp.exp(s)
            if limit is not None:
                p = jnp.where(mask_ref[...] <= limit, p, 0.0)
            sum_ref[rows, lanes] += p[:, :HD] + p[:, HD:]
            acc_ref[rows, lanes] += jnp.dot(p.astype(BF), value, preferred_element_type=F32)

    for (dx, dh), kv_ref in zip(deltas, kv_refs):
        base = ((x - (x ^ dx)) * 4 + head - (head ^ dh)) * 128

        @pl.loop(0, 6)
        def _(i):
            t, u = pair_of(i)
            unit(kv_ref, t, u, None)

        @pl.loop(0, 4)
        def _(t):
            unit(kv_ref, t, t, base)

    if last:

        @pl.loop(0, 4)
        def _(t):
            rows = pl.ds(pl.multiple_of(t * TILE, TILE), TILE)
            for h in range(2):
                lanes = slice(h * HD, (h + 1) * HD)
                total = jnp.sum(sum_ref[rows, lanes], axis=-1, keepdims=True)
                out = acc_ref[rows, lanes] / total
                att_ref[rows, lanes] = out
                low_ref[rows, lanes] = out.astype(BF)


def attend(meta, q, chunks, deltas, carry, last):
    first = carry is None
    rows = q.shape[0]
    f32 = jax.ShapeDtypeStruct((rows, 2 * HD), F32)
    low = jax.ShapeDtypeStruct((rows, 2 * HD), BF)
    scratch = [pltpu.VMEM((TILE, TILE), jnp.int32)]
    if last:
        scratch = [pltpu.VMEM((rows, 2 * HD), F32)] + scratch
    args = [meta, q, *chunks] + ([] if first else list(carry))
    work = len(deltas) * 10 * 512 * 256
    return pl.pallas_call(
        functools.partial(attend_kernel, first, last, deltas),
        in_specs=[SMEM] + [VMEM] * (len(args) - 1),
        out_specs=[VMEM] * (3 if last else 2),
        out_shape=[f32, low, f32] if last else [f32, f32],
        scratch_shapes=scratch,
        compiler_params=PARAMS,
        cost_estimate=pl.CostEstimate(flops=work * 512, bytes_accessed=6 << 20, transcendentals=work),
        name="attend",
    )(*args)


def attend_back_kernel(first, deltas, meta_ref, *refs):
    n = len(deltas)
    q_ref, do_ref, lse_ref, delta_ref = refs[:4]
    kv_refs = refs[4 : 4 + n]
    at = 4 + n
    if not first:
        dq_in = refs[at]
        at += 1
    dq_ref = refs[at]
    dkv_refs = refs[at + 1 : at + 1 + n]
    acc_ref, mask_ref = refs[at + 1 + n :]
    if first:
        dq_ref[...] = jnp.zeros_like(dq_ref)
    else:
        dq_ref[...] = dq_in[...]
    y, core, x, head = meta_ref[0], meta_ref[1], meta_ref[2], meta_ref[3]
    mask_ref[...] = spread(core, 0)
    nt = (((1,), (1,)), ((), ()))
    tn = (((0,), (0,)), ((), ()))

    def unit(kv_ref, t, u, limit):
        at_q = t ^ y
        rows = pl.ds(pl.multiple_of(at_q * TILE, TILE), TILE)
        cols = pl.ds(pl.multiple_of((u ^ y) * TILE, TILE), TILE)
        key = kv_ref[cols, :HD]
        value = kv_ref[cols, HD:]
        dk = dv = None
        for h in range(2):
            lanes = slice(h * HD, (h + 1) * HD)
            q = q_ref[rows, lanes]
            do = do_ref[rows, lanes]
            s = lax.dot_general(key, q, nt, preferred_element_type=F32)
            p = jnp.exp(s - lse_ref[at_q, h : h + 1, :])
            if limit is not None:
                p = jnp.where(mask_ref[...] <= limit, p, 0.0)
            dp = lax.dot_general(value, do, nt, preferred_element_type=F32)
            ds = (p * (dp - delta_ref[at_q, h : h + 1, :])).astype(BF)
            dv_h = jnp.dot(p.astype(BF), do, preferred_element_type=F32)
            dk_h = jnp.dot(ds, q, preferred_element_type=F32)
            dv = dv_h if dv is None else dv + dv_h
            dk = dk_h if dk is None else dk + dk_h
            dq_ref[rows, lanes] += lax.dot_general(ds, key, tn, preferred_element_type=F32)
        return cols, dk, dv

    for (dx, dh), kv_ref, dkv_ref in zip(deltas, kv_refs, dkv_refs):
        base = ((x - (x ^ dx)) * 4 + head - (head ^ dh)) * 128

        @pl.loop(0, 4)
        def _(t):
            cols, dk, dv = unit(kv_ref, t, t, base)
            acc_ref[cols, :HD] = dk
            acc_ref[cols, HD:] = dv

        @pl.loop(0, 6)
        def _(i):
            t, u = pair_of(i)
            cols, dk, dv = unit(kv_ref, t, u, None)
            acc_ref[cols, :HD] += dk
            acc_ref[cols, HD:] += dv

        dkv_ref[...] = acc_ref[...].astype(BF)


def attend_back(meta, q, do, lse, delta, chunks, deltas, carry):
    first = carry is None
    rows = q.shape[0]
    args = [meta, q, do, lse, delta, *chunks] + ([] if first else [carry])
    n = len(deltas)
    work = n * 10 * 512 * 256
    return pl.pallas_call(
        functools.partial(attend_back_kernel, first, deltas),
        in_specs=[SMEM] + [VMEM] * (len(args) - 1),
        out_specs=[VMEM] * (1 + n),
        out_shape=[jax.ShapeDtypeStruct((rows, 2 * HD), F32)] + [jax.ShapeDtypeStruct((rows, 2 * HD), BF)] * n,
        scratch_shapes=[pltpu.VMEM((rows, 2 * HD), F32), pltpu.VMEM((TILE, TILE), jnp.int32)],
        compiler_params=PARAMS,
        cost_estimate=pl.CostEstimate(flops=work * 1280, bytes_accessed=6 << 20, transcendentals=work),
        name="attend_back",
    )(*args)


def rms_parts(v):
    scale = lax.rsqrt(jnp.mean(v * v, axis=-1, keepdims=True) + EPS)
    return v * scale, scale


def rms_back(unit, scale, gain, grad):
    t = grad * gain
    return scale * (t - unit * jnp.mean(t * unit, axis=-1, keepdims=True))


def local(
    inputs, w_query, key_weight, value_weight, w_output, w_gate, w_up, w_down,
    gain_attn, gain_ffn, gain_query, gain_key, grad_outputs,
):
    sq, hd = lax.axis_index("seq"), lax.axis_index("head")
    y, x, core = lax.axis_index("y"), lax.axis_index("x"), lax.axis_index("core")
    zi = sq * 2 + hd
    tokens = inputs[0]
    count, width = tokens.shape
    rows = 8 * count
    meta = jnp.stack([y, core, x, hd]).astype(jnp.int32)

    slot = jnp.arange(8, dtype=jnp.int32)
    chunk = ((slot // 2) ^ y) * 16 + x * 4 + ((slot % 2) ^ core) * 2 + hd
    pos = (chunk[:, None] * count + jnp.arange(count, dtype=jnp.int32)[None, :]).reshape(-1)
    freqs = ROPE_BASE ** (-(jnp.arange(HD // 2, dtype=F32) * 2.0 / HD))
    angles = pos.astype(F32)[:, None] * freqs[None, :]
    cos, sin = jnp.cos(angles), jnp.sin(angles)
    cos = jnp.concatenate([cos, cos], axis=1)
    sin = jnp.concatenate([-sin, sin], axis=1)

    xg = gather_group(tokens).reshape(rows, width)

    def cut(w):
        return w.reshape(w.shape[0], 8, -1)

    cols = jnp.concatenate([cut(w_query), cut(key_weight), cut(value_weight), cut(w_gate), cut(w_up)], axis=2)
    cols = cols.transpose(1, 0, 2)
    cols = lax.all_to_all(cols, ("y", "core"), split_axis=0, concat_axis=0, tiled=True)
    n_qkv = 4 * HD
    n_ff = w_gate.shape[1] // 8

    def gather_rows(w):
        c = w.shape[-1]
        w = gather_x(w.reshape(4, 16, c), x, 1).reshape(256, c)
        return gather_z(w, zi).reshape(width, c)

    w_qkv = gather_rows(cols[:, :, :n_qkv])

    def index(s, h, yy, xx, c):
        return (((s * 2 + h) * 4 + yy) * 4 + xx) * 2 + c

    there = []
    for s in range(2):
        for h in range(2):
            for yy in range(4):
                for xx in range(4):
                    for c in range(2):
                        to = index(yy % 2, xx // 2, s * 2 + h, (xx % 2) * 2 + c, yy // 2)
                        there.append((index(s, h, yy, xx, c), to))
    back = [(b, a) for a, b in there]
    n_out = w_output.shape[0]
    tall = lax.ppermute(jnp.concatenate([w_output, w_down], axis=0), ALL, there)

    hidden, q, kv, raw = qkv_project(
        xg, gain_attn[None], w_qkv, gain_query[None], gain_key[None], cos, sin
    )

    kv_z = swap(kv, "head", 1)
    kvs = {(0, 0): kv, (0, 1): kv_z}
    for d in (1, 3, 2):
        kvs[(d, 0)] = swap(kv, "x", d)
    for d in (1, 3, 2):
        kvs[(d, 1)] = swap(kv_z, "x", d)

    w_gu = gather_rows(cols[:, :, n_qkv:])
    tall = gather_z(gather_x(tall, x, 0), zi)
    w_out = tall[:, :, :n_out].reshape(16 * n_out, width)
    w_dn = tall[:, :, n_out:].reshape(-1, width)
    w_out_all = gather_group(w_out).reshape(-1, width)
    dyg = gather_group(grad_outputs[0]).reshape(rows, width)

    carry = None
    orders = [((0, 0), (0, 1)), ((1, 0), (3, 0)), ((2, 0), (1, 1)), ((3, 1), (2, 1))]
    for step, deltas in enumerate(orders):
        carry = attend(meta, q, [kvs[d] for d in deltas], deltas, carry, step == len(orders) - 1)
    attended, attended_low, sums = carry
    lse = jnp.log(jnp.sum(sums.reshape(4, TILE, 2, HD), axis=-1)).transpose(0, 2, 1)

    own = exchange_group(attended_low.reshape(4, 2, count, 2 * HD))
    own = own.transpose(2, 0, 1, 3).reshape(count, -1)
    mid = tokens.astype(F32) + jnp.dot(own, w_out_all, preferred_element_type=F32)
    mid_unit, mid_scale = rms_parts(mid)
    h2 = (mid_unit * gain_ffn).astype(BF)
    h2g = gather_group(h2).reshape(rows, width)

    gu = jnp.dot(h2g, w_gu, preferred_element_type=F32)
    gate, up = gu[:, :n_ff], gu[:, n_ff:]
    sig = jax.nn.sigmoid(gate)
    act = (gate * sig * up).astype(BF)
    d_act = lax.dot_general(dyg, w_dn, (((1,), (1,)), ((), ())), preferred_element_type=F32)
    d_gate = (d_act * up * sig * (1.0 + gate * (1.0 - sig))).astype(BF)
    d_up = (d_act * gate * sig).astype(BF)
    d_gu = jnp.concatenate([d_gate, d_up], axis=1)
    d_h2 = lax.dot_general(d_gu, w_gu, (((1,), (1,)), ((), ())), preferred_element_type=F32)
    d_h2 = scatter_group(d_h2.reshape(4, 2, count, width))
    down = jnp.dot(act, w_dn, preferred_element_type=F32)
    result = (mid + scatter_group(down.reshape(4, 2, count, width))).astype(BF)

    grad_gain_ffn = jnp.sum(d_h2 * mid_unit, axis=0)
    d_mid = grad_outputs[0].astype(F32) + rms_back(mid_unit, mid_scale, gain_ffn, d_h2)
    d_mid_low = d_mid.astype(BF)
    d_own = lax.dot_general(d_mid_low, w_out_all, (((1,), (1,)), ((), ())), preferred_element_type=F32)
    d_own = d_own.astype(BF).reshape(count, 4, 2, 2 * HD).transpose(1, 2, 0, 3)
    d_o = exchange_group(d_own).reshape(rows, 2 * HD)
    delta = jnp.sum((d_o.astype(F32) * attended).reshape(4, TILE, 2, HD), axis=-1).transpose(0, 2, 1)

    tt = (((0,), (0,)), ((), ()))
    g_gu = lax.dot_general(h2g, d_gu, tt, preferred_element_type=F32)
    g_dn = lax.dot_general(act, dyg, tt, preferred_element_type=F32)
    d_mid_g = gather_group(d_mid_low).reshape(rows, width)
    g_out = lax.dot_general(attended_low, d_mid_g, tt, preferred_element_type=F32)

    def scatter_cols(g):
        c = g.shape[1]
        g = g.reshape(4, 4, 4, 16, c)
        g = reduce_slots([g[i] for i in range(4)], Z, zi)
        g = reduce_slots([g[:, i] for i in range(4)], "x", x)
        g = g.astype(BF).reshape(8, 8, c)
        return lax.all_to_all(g, ("y", "core"), split_axis=0, concat_axis=0, tiled=True).astype(F32)

    def scatter_rows(g):
        g = g.reshape(4, 4, -1, width)
        g = reduce_slots([g[i] for i in range(4)], Z, zi)
        return reduce_slots([g[i] for i in range(4)], "x", x)

    g_gu = scatter_cols(g_gu)
    g_tall = jnp.concatenate([scatter_rows(g_out), scatter_rows(g_dn)], axis=0).astype(BF)
    g_tall = lax.ppermute(g_tall, ALL, back).astype(F32)

    dkvs = {}
    carry = None
    orders = [((1, 1), (2, 1)), ((3, 1), (0, 1)), ((1, 0), (2, 0)), ((3, 0), (0, 0))]
    for deltas in orders:
        carry, *parts = attend_back(meta, q, d_o, lse, delta, [kvs[d] for d in deltas], deltas, carry)
        dkvs.update(zip(deltas, parts))
    far = dkvs[(0, 1)].astype(F32)
    for d in (1, 2, 3):
        far = far + swap(dkvs[(d, 1)], "x", d).astype(F32)
    near = dkvs[(0, 0)].astype(F32) + swap(far.astype(BF), "head", 1).astype(F32)
    for d in (1, 2, 3):
        near = near + swap(dkvs[(d, 0)], "x", d).astype(F32)
    d_raw, gain_part = qkv_back(
        carry.astype(BF), near.astype(BF), raw, gain_query[None], gain_key[None], cos, sin
    )

    d_h1 = lax.dot_general(d_raw, w_qkv, (((1,), (1,)), ((), ())), preferred_element_type=F32)
    d_h1 = scatter_group(d_h1.reshape(4, 2, count, width))
    g_qkv = lax.dot_general(hidden, d_raw, tt, preferred_element_type=F32)
    g_qkv = scatter_cols(g_qkv)
    unit, scale = rms_parts(tokens.astype(F32))
    grad_gain_attn = jnp.sum(d_h1 * unit, axis=0)
    grad_inputs = (d_mid + rms_back(unit, scale, gain_attn, d_h1)).astype(BF)

    gains = jnp.concatenate([grad_gain_attn, grad_gain_ffn, gain_part[0], gain_part[1]])
    gains = gains + swap(gains, "core", 1)
    for axis in ("y", "x", Z):
        gains = gains + swap(gains, axis, 1) + swap(gains, axis, 2) + swap(gains, axis, 3)

    def join(g, lo, hi):
        return g[:, :, lo:hi].transpose(1, 0, 2).reshape(g.shape[1], -1)

    return (
        result[None],
        grad_inputs[None],
        join(g_qkv, 0, 2 * HD),
        join(g_qkv, 2 * HD, 3 * HD),
        join(g_qkv, 3 * HD, 4 * HD),
        g_tall[:n_out],
        join(g_gu, 0, n_ff),
        join(g_gu, n_ff, 2 * n_ff),
        g_tall[n_out:],
        gains[:width],
        gains[width : 2 * width],
        gains[2 * width : 2 * width + HD],
        gains[2 * width + HD :],
    )


def solution(mesh):
    fine = Mesh(mesh.devices.reshape(2, 2, 4, 4, 2), ALL)
    token = P("seq", ("y", "x", "core", "head"), None)
    weight = P(ALL, None)
    in_specs = (token,) + (weight,) * 7 + (P(),) * 4 + (token,)
    out_specs = (token, token) + (weight,) * 7 + (P(),) * 4
    return jax.shard_map(local, mesh=fine, in_specs=in_specs, out_specs=out_specs, check_vma=False)
```

time: 4480 us -> 535 us (0.12)
  waiting for transfers between devices: 4070 us -> 126 us
  starting transfers between devices: 7.87 us -> 165 us
  blocking collectives: 123 us -> 0 us
  Pallas kernels: 0 us -> 120 us
  local copies, waits for them, and re-layouts: 122 us -> 39.2 us
  matrix products: 95.9 us -> 17.8 us
    reduce_scatter x7 -> x0, waiting for transfers between devices: 3120 us -> none  [the longest x1 647 us: local(): lax.psum_scatter(grad_w_query, ('seq', 'head', 'blk'), scatter_dimension=...]
    all_gather x9 -> x0, waiting for transfers between devices: 477 us -> none  [the longest x1 67.8 us: local(): lax.all_gather(value_weight, ('seq', 'head', 'blk'), axis=0, tiled=True)]
    unnamed x18 -> x0, waiting for transfers between devices: 446 us -> none
    ppermute x0 -> x108, starting transfers between devices: none -> 149 us  [the longest x106 148 us: swap(): return lax.ppermute(v, axis, [(i, i ^ m) for i in range(n)])]
    ppermute x0 -> x108, waiting for transfers between devices: none -> 126 us  [the longest x106 126 us: swap(): return lax.ppermute(v, axis, [(i, i ^ m) for i in range(n)])]
    pallas_call x0 -> x10, Pallas kernels: none -> 120 us  [the longest x4 64.6 us: attend_back(): pl.pallas_call(functools.partial(attend_back_kernel, first, deltas), in_s...]
    dot_general x28 -> x11, matrix products: 95.9 us -> 17.8 us  [the longest x1 2.51 us: local(): jnp.dot(own, w_out_all, preferred_element_type=F32)]
    psum x1 -> x0, blocking collectives: 68.1 us -> none  [local(): lax.psum((grad_gain_attn, grad_gain_ffn, grad_gain_query, grad_gain_key),...]
  transfers between devices with their start and end apart: 19 -> 111, of which waited for: 19 -> 42; matrix products, arithmetic and copies ran while one was open for 2% -> 18% of each run, Pallas kernels for 0% -> 23%
where the time goes in v1:
time: 535 us; the launch traced here: 524 us
  starting transfers between devices  165 us (31%)
  waiting for transfers between devices  126 us (24%)
  Pallas kernels  120 us (22%)
  other arithmetic  53.8 us (10%)
  local copies, waits for them, and re-layouts  39.2 us (7%)
  matrix products  17.8 us (3%)
    ppermute x106, starting transfers between devices, swap(): return lax.ppermute(v, axis, [(i, i ^ m) for i in range(n)])  148 us
    ppermute x106, waiting for transfers between devices, swap(): return lax.ppermute(v, axis, [(i, i ^ m) for i in range(n)])  126 us
    pallas_call x4, Pallas kernels, attend_back(): pl.pallas_call(functools.partial(attend_back_kernel, first, deltas), in_s...  64.6 us
    pallas_call x4, Pallas kernels, attend(): pl.pallas_call(functools.partial(attend_kernel, first, last, deltas), in_...  47.8 us
    another operation x10, other arithmetic, gather_group(): return jnp.stack([w, swap(w, 'core', 1)], axis=1)  15.3 us
    unnamed x115, local copies, waits for them, and re-layouts  14.3 us
  transfers between devices with their start and end apart: 111, of which 42 were waited for; matrix products, arithmetic and copies ran while one was open for 18% of the time, Pallas kernels for 23%

profile of v1, /device:TPU:0, one launch (start us, length us, event | category | flops | bytes accessed | tf_op | source)
XLA Modules:
  0.0 524.5 jit_solution(13786585690780929007)
XLA Ops:
  0.6 3.4 collective-permute-start.1
  13.0 8.6 %all-to-all-start = ((bf16[8,8,1280]{2,1,0:T(8,128)(2,1)}), bf16[8,8,1280]{2,1,0:T(8,128)(2,1)S(1)}, u32[]{:S(2)}, u32[]{:S(2)}) async-start(bf16[8,8,1280]{2,1,0:T(8,128)(2,1)} %bitcast.17), calls=%async_computation | async-start | bytes 327680 | tf_op jit(solution)/shard_map/all_to_all | solution.py:384
  36.4 3.0 collective-permute-start.2
  50.7 6.5 %collective-permute-done.26 = bf16[4,40,1024]{2,1,0:T(8,128)(2,1)S(1)} collective-permute-done((bf16[4,40,1024]{2,1,0:T(8,128)(2,1)S(1)}, bf16[4,40,1024]{2,1,0:T(8,128)(2,1)S(1)}, u32[]{:S(2)}, u32[]{:S(2)}) %collective-permute-start.26) | collective-permute-done | bytes 327712 | tf_op jit(solution)/shard_map/ppermute | solution.py:24
  57.2 4.6 collective-permute-done.25
  62.1 5.8 %collective-permute-start.30 = (bf16[256,1024]{1,0:T(8,128)(2,1)S(1)}, bf16[256,1024]{1,0:T(8,128)(2,1)S(1)}, u32[]{:S(2)}, u32[]{:S(2)}) collective-permute-start(bf16[256,1024]{1,0:T(8,128)(2,1)S(1)} %bitcast.564), channel_id=1, source_target_pairs={{0,24},{8,16},{16,8},{24,0},{1,25},{9,17},{17,9},{25,1},{2,26},{10... | collective-permute-start | bytes 1572872 | tf_op jit(solution)/shard_map/ppermute | solution.py:24
  71.7 5.4 %qkv_project.1 = (bf16[1024,1024]{1,0:T(8,128)(2,1)}, bf16[1024,256]{1,0:T(8,128)(2,1)S(1)}, bf16[1024,256]{1,0:T(8,128)(2,1)S(1)}, f32[1024,384]{1,0:T(8,128)S(1)}) custom-call(bf16[1024,1024]{1,0:T(8,128)(2,1)} %bitcast.553, f32[1,1024]{1,0:T(1,128)S(1)} %bitcast.536, bf16[1024,512]{1,0:T(8,128)(2,1)S(1)} %bitcast.528, f32[1,128]{1,0:T(1,128)S(1)} %bitcast.545, ...), custom_call_target="tpu_custom_call" | custom-call | flops 1073741824 | bytes 8388608 | tf_op jit(solution)/shard_map/qkv_project/pallas_call | solution.py:97
  78.8 5.5 %collective-permute-done.30 = bf16[256,1024]{1,0:T(8,128)(2,1)S(1)} collective-permute-done((bf16[256,1024]{1,0:T(8,128)(2,1)S(1)}, bf16[256,1024]{1,0:T(8,128)(2,1)S(1)}, u32[]{:S(2)}, u32[]{:S(2)}) %collective-permute-start.30) | collective-permute-done | bytes 524320 | tf_op jit(solution)/shard_map/ppermute | solution.py:24
  88.3 7.6 %collective-permute-done.10.refs_2_.refs_5_ = bf16[1024,256]{1,0:T(8,128)(2,1)S(1)} collective-permute-done((bf16[1024,256]{1,0:T(8,128)(2,1)S(1)}, bf16[1024,256]{1,0:T(8,128)(2,1)S(1)}, u32[]{:S(2)}, u32[]{:S(2)}) %collective-permute-start.10) | collective-permute-done | bytes 524320 | tf_op jit(solution)/shard_map/ppermute | solution.py:24
  98.0 4.2 collective-permute-start.12
  102.3 11.5 %attend.4 = (f32[1024,256]{1,0:T(8,128)S(1)}, f32[1024,256]{1,0:T(8,128)S(1)}) custom-call(s32[4]{0:T(128)S(1)} %pad_add_fusion.meta_ref, bf16[1024,256]{1,0:T(8,128)(2,1)S(1)} %get-tuple-element.40.refs_0_, bf16[1024,256]{1,0:T(8,128)(2,1)S(1)} %get-tuple-element.41.refs_1_.refs_5_, bf16[1024,256]{1,0:T(8,128)(2,1)S(1)} %collective-permute-done.10.refs_2_.refs_5_), custom_call_target="tpu_custom_call" | custom-call | flops 1342177280 | bytes 6291456 | tf_op jit(solution)/shard_map/attend/pallas_call | solution.py:253
  113.9 11.5 %attend.5 = (f32[1024,256]{1,0:T(8,128)S(1)}, f32[1024,256]{1,0:T(8,128)S(1)}) custom-call(s32[4]{0:T(128)S(1)} %pad_add_fusion.meta_ref, bf16[1024,256]{1,0:T(8,128)(2,1)S(1)} %get-tuple-element.40.refs_0_, bf16[1024,256]{1,0:T(8,128)(2,1)S(1)} %collective-permute-done.15.refs_1_.refs_4_, bf16[1024,256]{1,0:T(8,128)(2,1)S(1)} %collective-permute-done.16.refs_2_.refs_4_, ...), custom_call_target="tpu_custom_call" | custom-call | flops 1342177280 | bytes 6291456 | tf_op jit(solution)/shard_map/attend/pallas_call | solution.py:253
  125.5 11.5 %attend.6 = (f32[1024,256]{1,0:T(8,128)S(1)}, f32[1024,256]{1,0:T(8,128)S(1)}) custom-call(s32[4]{0:T(128)S(1)} %pad_add_fusion.meta_ref, bf16[1024,256]{1,0:T(8,128)(2,1)S(1)} %get-tuple-element.40.refs_0_, bf16[1024,256]{1,0:T(8,128)(2,1)S(1)} %collective-permute-done.13.refs_1_.refs_5_, bf16[1024,256]{1,0:T(8,128)(2,1)S(1)} %collective-permute-done.14.refs_2_.refs_4_, ...), custom_call_target="tpu_custom_call" | custom-call | flops 1342177280 | bytes 6291456 | tf_op jit(solution)/shard_map/attend/pallas_call | solution.py:253
  138.1 13.2 %attend.7 = (f32[1024,256]{1,0:T(8,128)S(1)}, bf16[1024,256]{1,0:T(8,128)(2,1)S(1)}, f32[1024,256]{1,0:T(8,128)S(1)}) custom-call(s32[4]{0:T(128)S(1)} %pad_add_fusion.meta_ref, bf16[1024,256]{1,0:T(8,128)(2,1)S(1)} %get-tuple-element.40.refs_0_, bf16[1024,256]{1,0:T(8,128)(2,1)S(1)} %collective-permute-done.11.refs_1_.refs_4_, ...), custom_call_target="tpu_custom_call" | custom-call | flops 1342177280 | bytes 6291456 | tf_op jit(solution)/shard_map/attend/pallas_call | solution.py:253
  151.9 4.6 collective-permute-start.37
  158.4 3.4 collective-permute-done.37
  163.9 3.1 collective-permute-start.19
  168.3 3.4 collective-permute-done.19
  175.1 3.2 collective-permute-start.33
  179.9 5.8 %collective-permute-done.33 = bf16[128,1024]{1,0:T(8,128)(2,1)S(1)} collective-permute-done((bf16[128,1024]{1,0:T(8,128)(2,1)S(1)}, bf16[128,1024]{1,0:T(8,128)(2,1)S(1)}, u32[]{:S(2)}, u32[]{:S(2)}) %collective-permute-start.33) | collective-permute-done | bytes 262176 | tf_op jit(solution)/shard_map/ppermute | solution.py:24
  185.7 2.6 collective-permute-start.40
  195.1 6.4 %collective-permute-done.39 = bf16[256,768]{1,0:T(8,128)(2,1)S(1)} collective-permute-done((bf16[256,768]{1,0:T(8,128)(2,1)S(1)}, bf16[256,768]{1,0:T(8,128)(2,1)S(1)}, u32[]{:S(2)}, u32[]{:S(2)}) %collective-permute-start.39) | collective-permute-done | bytes 393248 | tf_op jit(solution)/shard_map/ppermute | solution.py:24
  204.8 2.7 reshape.410
  207.5 3.2 reduce_sum.75
  213.9 4.7 pad_maximum_fusion
  228.2 2.8 collective-permute-start.86
  233.1 2.8 collective-permute-start.93
  247.0 3.4 collective-permute-done.93
  251.5 5.1 collective-permute-done.94
  256.9 9.6 %collective-permute-start.96 = (bf16[4,16,768]{2,1,0:T(8,128)(2,1)S(1)}, bf16[4,16,768]{2,1,0:T(8,128)(2,1)S(1)}, u32[]{:S(2)}, u32[]{:S(2)}) collective-permute-start(bf16[4,16,768]{2,1,0:T(8,128)(2,1)S(1)} %fusion.71), channel_id=1, source_target_pairs={{0,6},{2,4},{4,2},{6,0},{1,7},{3,5},{5,3},{7,1},{8,14},{10,12},{12... | collective-permute-start | bytes 294920 | tf_op jit(solution)/shard_map/ppermute | solution.py:24
  275.7 3.9 all-to-all-start.2
  279.6 3.8 fusion.108
  286.4 2.7 collective-permute-start.53
  293.8 7.6 %collective-permute-done.53 = bf16[128,1024]{1,0:T(8,128)(2,1)} collective-permute-done((bf16[128,1024]{1,0:T(8,128)(2,1)}, bf16[128,1024]{1,0:T(8,128)(2,1)}, u32[]{:S(2)}, u32[]{:S(2)}) %collective-permute-start.53) | collective-permute-done | bytes 262176 | tf_op jit(solution)/shard_map/ppermute | solution.py:24
  301.4 2.6 collective-permute-done.52
  308.8 3.0 collective-permute-start.75
  316.8 4.2 fusion.110
  322.2 2.9 collective-permute-start.56
  325.2 2.8 fusion.99
  328.1 2.9 collective-permute-done.57
  332.3 2.7 reshape.411
  335.1 3.3 reduce_sum.76
  342.7 16.1 %attend_back.4 = (f32[1024,256]{1,0:T(8,128)S(1)}, bf16[1024,256]{1,0:T(8,128)(2,1)S(1)}, bf16[1024,256]{1,0:T(8,128)(2,1)S(1)}) custom-call(s32[4]{0:T(128)S(1)} %pad_add_fusion.meta_ref, bf16[1024,256]{1,0:T(8,128)(2,1)S(1)} %copy-done.9, bf16[1024,256]{1,0:T(8,128)(2,1)S(1)} %bitcast.531, f32[4,2,256]{2,1,0:T(2,128)S(1)} %bitcast.541, ...), custom_call_target="tpu_custom_call" | custom-call | flops 3355443200 | bytes 6291456 | tf_op jit(solution)/shard_map/attend_back/pallas_call | solution.py:334
  358.9 16.2 %attend_back.5 = (f32[1024,256]{1,0:T(8,128)S(1)}, bf16[1024,256]{1,0:T(8,128)(2,1)S(1)}, bf16[1024,256]{1,0:T(8,128)(2,1)S(1)}) custom-call(s32[4]{0:T(128)S(1)} %pad_add_fusion.meta_ref, bf16[1024,256]{1,0:T(8,128)(2,1)S(1)} %copy-done.10, bf16[1024,256]{1,0:T(8,128)(2,1)S(1)} %bitcast.532, f32[4,2,256]{2,1,0:T(2,128)S(1)} %bitcast.542, ...), custom_call_target="tpu_custom_call" | custom-call | flops 3355443200 | bytes 6291456 | tf_op jit(solution)/shard_map/attend_back/pallas_call | solution.py:334
  375.1 2.6 collective-permute-start.60
  380.0 16.2 %attend_back.6 = (f32[1024,256]{1,0:T(8,128)S(1)}, bf16[1024,256]{1,0:T(8,128)(2,1)S(1)}, bf16[1024,256]{1,0:T(8,128)(2,1)S(1)}) custom-call(s32[4]{0:T(128)S(1)} %pad_add_fusion.meta_ref, bf16[1024,256]{1,0:T(8,128)(2,1)S(1)} %copy-done.10, bf16[1024,256]{1,0:T(8,128)(2,1)S(1)} %bitcast.533, f32[4,2,256]{2,1,0:T(2,128)S(1)} %bitcast.543, ...), custom_call_target="tpu_custom_call" | custom-call | flops 3355443200 | bytes 6291456 | tf_op jit(solution)/shard_map/attend_back/pallas_call | solution.py:334
  396.2 16.1 %attend_back.7 = (f32[1024,256]{1,0:T(8,128)S(1)}, bf16[1024,256]{1,0:T(8,128)(2,1)S(1)}, bf16[1024,256]{1,0:T(8,128)(2,1)S(1)}) custom-call(s32[4]{0:T(128)S(1)} %pad_add_fusion.meta_ref, bf16[1024,256]{1,0:T(8,128)(2,1)S(1)} %copy-done.10, bf16[1024,256]{1,0:T(8,128)(2,1)S(1)} %bitcast.534, f32[4,2,256]{2,1,0:T(2,128)S(1)} %bitcast.544, ...), custom_call_target="tpu_custom_call" | custom-call | flops 3355443200 | bytes 6291456 | tf_op jit(solution)/shard_map/attend_back/pallas_call | solution.py:334
  412.4 2.6 collective-permute-start.64
  420.0 2.9 collective-permute-start.80
  423.0 4.7 collective-permute-done.64
  432.0 6.8 %collective-permute-done.63 = bf16[1024,256]{1,0:T(8,128)(2,1)S(1)} collective-permute-done((bf16[1024,256]{1,0:T(8,128)(2,1)S(1)}, bf16[1024,256]{1,0:T(8,128)(2,1)S(1)}, u32[]{:S(2)}, u32[]{:S(2)}) %collective-permute-start.63) | collective-permute-done | bytes 524320 | tf_op jit(solution)/shard_map/ppermute | solution.py:24
  439.2 2.6 qkv_back.1
  443.4 2.6 collective-permute-start.83
  449.5 2.9 collective-permute-start.70
  455.0 4.5 collective-permute-done.70
  461.6 6.2 %collective-permute-done.71 = bf16[4,4,16,512]{3,2,1,0:T(8,128)(2,1)S(1)} collective-permute-done((bf16[4,4,16,512]{3,2,1,0:T(8,128)(2,1)S(1)}, bf16[4,4,16,512]{3,2,1,0:T(8,128)(2,1)S(1)}, u32[]{:S(2)}, u32[]{:S(2)}) %collective-permute-start.71) | collective-permute-done | bytes 262176 | tf_op jit(solution)/shard_map/ppermute | solution.py:24
  470.9 2.5 collective-permute-start.68
  474.6 3.4 collective-permute-done.66
  478.1 5.8 %collective-permute-done.68 = bf16[128,1024]{1,0:T(8,128)(2,1)S(1)} collective-permute-done((bf16[128,1024]{1,0:T(8,128)(2,1)S(1)}, bf16[128,1024]{1,0:T(8,128)(2,1)S(1)}, u32[]{:S(2)}, u32[]{:S(2)}) %collective-permute-start.68) | collective-permute-done | bytes 262176 | tf_op jit(solution)/shard_map/ppermute | solution.py:24
  490.5 3.5 all-to-all-start.1
  494.7 3.2 collective-permute-start.101
  501.6 2.7 collective-permute-start.45
  511.3 2.7 collective-permute-done.103
  514.5 3.2 collective-permute-start.107
  (408 shorter events, 179.9 us)
Async XLA Ops:
  0.6 40.8 %collective-permute-start.1 = (bf16[128,1024]{1,0:T(8,128)(2,1)}, bf16[128,1024]{1,0:T(8,128)(2,1)S(1)}, u32[]{:S(2)}, u32[]{:S(2)}) collective-permute-start(bf16[128,1024]{1,0:T(8,128)(2,1)} %bitcast.554), channel_id=1, source_target_pairs={{0,16},{8,24},{16,0},{24,8},{1,17},{9,25},{17,1},{25,9},{2,18},{10... | collective-permute-start | bytes 786440 | tf_op jit(solution)/shard_map/ppermute | solution.py:24
  4.0 40.1 %collective-permute-start = (bf16[128,1024]{1,0:T(8,128)(2,1)}, bf16[128,1024]{1,0:T(8,128)(2,1)}, u32[]{:S(2)}, u32[]{:S(2)}) collective-permute-start(bf16[128,1024]{1,0:T(8,128)(2,1)} %bitcast.555), channel_id=1, source_target_pairs={{0,8},{8,0},{16,24},{24,16},{1,9},{9,1},{17,25},{25,17},{2,10},{10... | collective-permute-start | bytes 786440 | tf_op jit(solution)/shard_map/ppermute | solution.py:24
  5.5 18.2 %collective-permute-start.21 = (bf16[40,1024]{1,0:T(8,128)(2,1)S(1)}, bf16[40,1024]{1,0:T(8,128)(2,1)S(1)}, u32[]{:S(2)}, u32[]{:S(2)}) collective-permute-start(bf16[40,1024]{1,0:T(8,128)(2,1)S(1)} %pad_maximum_fusion.25), channel_id=1, source_target_pairs={{0,0},{1,2},{2,4},{3,6},{4,32},{5,34},{6,36},{7,38},{8,64},{9,66},... | collective-permute-start | bytes 245768 | tf_op jit(solution)/shard_map/ppermute | solution.py:408
  13.0 16.0 %all-to-all-start = ((bf16[8,8,1280]{2,1,0:T(8,128)(2,1)}), bf16[8,8,1280]{2,1,0:T(8,128)(2,1)S(1)}, u32[]{:S(2)}, u32[]{:S(2)}) async-start(bf16[8,8,1280]{2,1,0:T(8,128)(2,1)} %bitcast.17), calls=%async_computation | async-start | bytes 327680 | tf_op jit(solution)/shard_map/all_to_all | solution.py:384
  40.8 16.4 %collective-permute-start.26 = (bf16[4,40,1024]{2,1,0:T(8,128)(2,1)S(1)}, bf16[4,40,1024]{2,1,0:T(8,128)(2,1)S(1)}, u32[]{:S(2)}, u32[]{:S(2)}) collective-permute-start(bf16[4,40,1024]{2,1,0:T(8,128)(2,1)S(1)} %pad_maximum_fusion.21), channel_id=1, source_target_pairs={{0,64},{32,96},{64,0},{96,32},{1,65},{33,97},{65,1},{97,33},{2,66}... | collective-permute-start | bytes 983048 | tf_op jit(solution)/shard_map/ppermute | solution.py:24
  41.5 20.3 %collective-permute-start.25 = (bf16[4,40,1024]{2,1,0:T(8,128)(2,1)S(1)}, bf16[4,40,1024]{2,1,0:T(8,128)(2,1)S(1)}, u32[]{:S(2)}, u32[]{:S(2)}) collective-permute-start(bf16[4,40,1024]{2,1,0:T(8,128)(2,1)S(1)} %pad_maximum_fusion.21), channel_id=1, source_target_pairs={{0,96},{32,64},{64,32},{96,0},{1,97},{33,65},{65,33},{97,1},{2,98}... | collective-permute-start | bytes 983048 | tf_op jit(solution)/shard_map/ppermute | solution.py:24
  44.1 23.8 %collective-permute-start.9 = (bf16[256,512]{1,0:T(8,128)(2,1)S(1)}, bf16[256,512]{1,0:T(8,128)(2,1)S(1)}, u32[]{:S(2)}, u32[]{:S(2)}) collective-permute-start(bf16[256,512]{1,0:T(8,128)(2,1)S(1)} %bitcast.582), channel_id=1, source_target_pairs={{0,32},{32,0},{64,96},{96,64},{1,33},{33,1},{65,97},{97,65},{2,34}... | collective-permute-start | bytes 786440 | tf_op jit(solution)/shard_map/ppermute | solution.py:24
  45.6 23.4 %collective-permute-start.8 = (bf16[256,512]{1,0:T(8,128)(2,1)S(1)}, bf16[256,512]{1,0:T(8,128)(2,1)S(1)}, u32[]{:S(2)}, u32[]{:S(2)}) collective-permute-start(bf16[256,512]{1,0:T(8,128)(2,1)S(1)} %bitcast.583), channel_id=1, source_target_pairs={{0,64},{32,96},{64,0},{96,32},{1,65},{33,97},{65,1},{97,33},{2,66}... | collective-permute-start | bytes 786440 | tf_op jit(solution)/shard_map/ppermute | solution.py:24
  50.0 19.7 %collective-permute-start.7 = (bf16[256,512]{1,0:T(8,128)(2,1)S(1)}, bf16[256,512]{1,0:T(8,128)(2,1)S(1)}, u32[]{:S(2)}, u32[]{:S(2)}) collective-permute-start(bf16[256,512]{1,0:T(8,128)(2,1)S(1)} %bitcast.584), channel_id=1, source_target_pairs={{0,96},{32,64},{64,32},{96,0},{1,97},{33,65},{65,33},{97,1},{2,98}... | collective-permute-start | bytes 786440 | tf_op jit(solution)/shard_map/ppermute | solution.py:24
  57.2 12.8 %collective-permute-start.3 = (bf16[4,128,1024]{2,1,0:T(8,128)(2,1)S(1)}, bf16[4,128,1024]{2,1,0:T(8,128)(2,1)S(1)}, u32[]{:S(2)}, u32[]{:S(2)}) collective-permute-start(bf16[4,128,1024]{2,1,0:T(8,128)(2,1)S(1)} %get-tuple-element.123), channel_id=1, source_target_pairs={{0,1},{1,0},{2,3},{3,2},{4,5},{5,4},{6,7},{7,6},{8,9},{9,8},{10,11... | collective-permute-start | bytes 3145736 | tf_op jit(solution)/shard_map/ppermute | solution.py:24
  62.1 22.2 %collective-permute-start.30 = (bf16[256,1024]{1,0:T(8,128)(2,1)S(1)}, bf16[256,1024]{1,0:T(8,128)(2,1)S(1)}, u32[]{:S(2)}, u32[]{:S(2)}) collective-permute-start(bf16[256,1024]{1,0:T(8,128)(2,1)S(1)} %bitcast.564), channel_id=1, source_target_pairs={{0,24},{8,16},{16,8},{24,0},{1,25},{9,17},{17,9},{25,1},{2,26},{10... | collective-permute-start | bytes 1572872 | tf_op jit(solution)/shard_map/ppermute | solution.py:24
  67.9 17.2 %collective-permute-start.29 = (bf16[256,1024]{1,0:T(8,128)(2,1)S(1)}, bf16[256,1024]{1,0:T(8,128)(2,1)S(1)}, u32[]{:S(2)}, u32[]{:S(2)}) collective-permute-start(bf16[256,1024]{1,0:T(8,128)(2,1)S(1)} %bitcast.565), channel_id=1, source_target_pairs={{0,16},{8,24},{16,0},{24,8},{1,17},{9,25},{17,1},{25,9},{2,18},{10... | collective-permute-start | bytes 1572872 | tf_op jit(solution)/shard_map/ppermute | solution.py:24
  69.0 16.1 %collective-permute-start.28 = (bf16[256,1024]{1,0:T(8,128)(2,1)S(1)}, bf16[256,1024]{1,0:T(8,128)(2,1)S(1)}, u32[]{:S(2)}, u32[]{:S(2)}) collective-permute-start(bf16[256,1024]{1,0:T(8,128)(2,1)S(1)} %bitcast.566), channel_id=1, source_target_pairs={{0,8},{8,0},{16,24},{24,16},{1,9},{9,1},{17,25},{25,17},{2,10},{10... | collective-permute-start | bytes 1572872 | tf_op jit(solution)/shard_map/ppermute | solution.py:24
  77.1 20.9 %collective-permute-start.16 = (bf16[1024,256]{1,0:T(8,128)(2,1)S(1)}, bf16[1024,256]{1,0:T(8,128)(2,1)S(1)}, u32[]{:S(2)}, u32[]{:S(2)}) collective-permute-start(bf16[1024,256]{1,0:T(8,128)(2,1)S(1)} %get-tuple-element.41.refs_1_.refs_5_), channel_id=1, source_target_pairs={{0,6},{2,4},{4,2},{6,0},{1,7},{3,5},{5,3},{7,1},{8,14},{10,12},{12... | collective-permute-start | bytes 1572872 | tf_op jit(solution)/shard_map/ppermute | solution.py:24
  78.8 23.4 %collective-permute-start.15 = (bf16[1024,256]{1,0:T(8,128)(2,1)S(1)}, bf16[1024,256]{1,0:T(8,128)(2,1)S(1)}, u32[]{:S(2)}, u32[]{:S(2)}) collective-permute-start(bf16[1024,256]{1,0:T(8,128)(2,1)S(1)} %get-tuple-element.41.refs_1_.refs_5_), channel_id=1, source_target_pairs={{0,2},{2,0},{4,6},{6,4},{1,3},{3,1},{5,7},{7,5},{8,10},{10,8},{12,... | collective-permute-start | bytes 1572872 | tf_op jit(solution)/shard_map/ppermute | solution.py:24
  86.8 85.6 %collective-permute-start.31 = (bf16[4,256,1024]{2,1,0:T(8,128)(2,1)}, bf16[4,256,1024]{2,1,0:T(8,128)(2,1)}, u32[]{:S(2)}, u32[]{:S(2)}) collective-permute-start(bf16[4,256,1024]{2,1,0:T(8,128)(2,1)} %get-tuple-element.89), channel_id=1, source_target_pairs={{0,1},{1,0},{2,3},{3,2},{4,5},{5,4},{6,7},{7,6},{8,9},{9,8},{10,11... | collective-permute-start | bytes 6291464 | tf_op jit(solution)/shard_map/ppermute | solution.py:24
  86.8 38.6 %collective-permute-start.13 = (bf16[1024,256]{1,0:T(8,128)(2,1)S(1)}, bf16[1024,256]{1,0:T(8,128)(2,1)S(1)}, u32[]{:S(2)}, u32[]{:S(2)}) collective-permute-start(bf16[1024,256]{1,0:T(8,128)(2,1)S(1)} %get-tuple-element.41.refs_1_.refs_5_), channel_id=1, source_target_pairs={{0,4},{2,6},{4,0},{6,2},{1,5},{3,7},{5,1},{7,3},{8,12},{10,14},{12... | collective-permute-start | bytes 1572872 | tf_op jit(solution)/shard_map/ppermute | solution.py:24
  95.9 29.5 %collective-permute-start.14 = (bf16[1024,256]{1,0:T(8,128)(2,1)S(1)}, bf16[1024,256]{1,0:T(8,128)(2,1)S(1)}, u32[]{:S(2)}, u32[]{:S(2)}) collective-permute-start(bf16[1024,256]{1,0:T(8,128)(2,1)S(1)} %collective-permute-done.10.refs_2_.refs_5_), channel_id=1, source_target_pairs={{0,2},{2,0},{4,6},{6,4},{1,3},{3,1},{5,7},{7,5},{8,10},{10,8},{12,... | collective-permute-start | bytes 1572872 | tf_op jit(solution)/shard_map/ppermute | solution.py:24
  98.0 40.1 %collective-permute-start.12 = (bf16[1024,256]{1,0:T(8,128)(2,1)S(1)}, bf16[1024,256]{1,0:T(8,128)(2,1)S(1)}, u32[]{:S(2)}, u32[]{:S(2)}) collective-permute-start(bf16[1024,256]{1,0:T(8,128)(2,1)S(1)} %collective-permute-done.10.refs_2_.refs_5_), channel_id=1, source_target_pairs={{0,4},{2,6},{4,0},{6,2},{1,5},{3,7},{5,1},{7,3},{8,12},{10,14},{12... | collective-permute-start | bytes 1572872 | tf_op jit(solution)/shard_map/ppermute | solution.py:24
  102.2 35.8 %collective-permute-start.11 = (bf16[1024,256]{1,0:T(8,128)(2,1)S(1)}, bf16[1024,256]{1,0:T(8,128)(2,1)S(1)}, u32[]{:S(2)}, u32[]{:S(2)}) collective-permute-start(bf16[1024,256]{1,0:T(8,128)(2,1)S(1)} %collective-permute-done.10.refs_2_.refs_5_), channel_id=1, source_target_pairs={{0,6},{2,4},{4,2},{6,0},{1,7},{3,5},{5,3},{7,1},{8,14},{10,12},{12... | collective-permute-start | bytes 1572872 | tf_op jit(solution)/shard_map/ppermute | solution.py:24
  151.5 26.8 %collective-permute-start.47 = (bf16[128,1024]{1,0:T(8,128)(2,1)S(1)}, bf16[128,1024]{1,0:T(8,128)(2,1)S(1)}, u32[]{:S(2)}, u32[]{:S(2)}) collective-permute-start(bf16[128,1024]{1,0:T(8,128)(2,1)S(1)} %bitcast.561), channel_id=1, source_target_pairs={{0,16},{8,24},{16,0},{24,8},{1,17},{9,25},{17,1},{25,9},{2,18},{10... | collective-permute-start | bytes 786440 | tf_op jit(solution)/shard_map/ppermute | solution.py:24
  171.7 21.0 %collective-permute-start.41 = (bf16[256,768]{1,0:T(8,128)(2,1)S(1)}, bf16[256,768]{1,0:T(8,128)(2,1)S(1)}, u32[]{:S(2)}, u32[]{:S(2)}) collective-permute-start(bf16[256,768]{1,0:T(8,128)(2,1)S(1)} %bitcast.576), channel_id=1, source_target_pairs={{0,32},{32,0},{64,96},{96,64},{1,33},{33,1},{65,97},{97,65},{2,34}... | collective-permute-start | bytes 1179656 | tf_op jit(solution)/shard_map/ppermute | solution.py:24
  179.5 23.5 %collective-permute-start.49 = (bf16[4,128,1024]{2,1,0:T(8,128)(2,1)S(1)}, bf16[4,128,1024]{2,1,0:T(8,128)(2,1)S(1)}, u32[]{:S(2)}, u32[]{:S(2)}) collective-permute-start(bf16[4,128,1024]{2,1,0:T(8,128)(2,1)S(1)} %get-tuple-element.112), channel_id=1, source_target_pairs={{0,1},{1,0},{2,3},{3,2},{4,5},{5,4},{6,7},{7,6},{8,9},{9,8},{10,11... | collective-permute-start | bytes 3145736 | tf_op jit(solution)/shard_map/ppermute | solution.py:24
  188.3 13.1 %collective-permute-start.39 = (bf16[256,768]{1,0:T(8,128)(2,1)S(1)}, bf16[256,768]{1,0:T(8,128)(2,1)S(1)}, u32[]{:S(2)}, u32[]{:S(2)}) collective-permute-start(bf16[256,768]{1,0:T(8,128)(2,1)S(1)} %bitcast.578), channel_id=1, source_target_pairs={{0,96},{32,64},{64,32},{96,0},{1,97},{33,65},{65,33},{97,1},{2,98}... | collective-permute-start | bytes 1179656 | tf_op jit(solution)/shard_map/ppermute | solution.py:24
  191.7 26.9 %collective-permute-start.35 = (bf16[4,128,1024]{2,1,0:T(8,128)(2,1)}, bf16[4,128,1024]{2,1,0:T(8,128)(2,1)}, u32[]{:S(2)}, u32[]{:S(2)}) collective-permute-start(bf16[4,128,1024]{2,1,0:T(8,128)(2,1)} %get-tuple-element.117), channel_id=1, source_target_pairs={{0,1},{1,0},{2,3},{3,2},{4,5},{5,4},{6,7},{7,6},{8,9},{9,8},{10,11... | collective-permute-start | bytes 3145736 | tf_op jit(solution)/shard_map/ppermute | solution.py:24
  228.2 16.0 %collective-permute-start.86 = (bf16[4,24,1024]{2,1,0:T(8,128)(2,1)S(1)}, bf16[4,24,1024]{2,1,0:T(8,128)(2,1)S(1)}, u32[]{:S(2)}, u32[]{:S(2)}) collective-permute-start(bf16[4,24,1024]{2,1,0:T(8,128)(2,1)S(1)} %bitcast.615), channel_id=1, source_target_pairs={{0,96},{32,64},{64,32},{96,0},{1,97},{33,65},{65,33},{97,1},{2,98}... | collective-permute-start | bytes 589832 | tf_op jit(solution)/shard_map/ppermute | solution.py:24
  231.0 15.2 %collective-permute-start.85 = (bf16[4,24,1024]{2,1,0:T(8,128)(2,1)S(1)}, bf16[4,24,1024]{2,1,0:T(8,128)(2,1)S(1)}, u32[]{:S(2)}, u32[]{:S(2)}) collective-permute-start(bf16[4,24,1024]{2,1,0:T(8,128)(2,1)S(1)} %bitcast.614), channel_id=1, source_target_pairs={{0,32},{32,0},{64,96},{96,64},{1,33},{33,1},{65,97},{97,65},{2,34}... | collective-permute-start | bytes 589832 | tf_op jit(solution)/shard_map/ppermute | solution.py:24
  231.0 15.3 %collective-permute-start.87 = (bf16[4,24,1024]{2,1,0:T(8,128)(2,1)S(1)}, bf16[4,24,1024]{2,1,0:T(8,128)(2,1)S(1)}, u32[]{:S(2)}, u32[]{:S(2)}) collective-permute-start(bf16[4,24,1024]{2,1,0:T(8,128)(2,1)S(1)} %bitcast.613), channel_id=1, source_target_pairs={{0,64},{32,96},{64,0},{96,32},{1,65},{33,97},{65,1},{97,33},{2,66}... | collective-permute-start | bytes 589832 | tf_op jit(solution)/shard_map/ppermute | solution.py:24
  233.1 17.2 %collective-permute-start.93 = (bf16[4,4,16,768]{3,2,1,0:T(8,128)(2,1)S(1)}, bf16[4,4,16,768]{3,2,1,0:T(8,128)(2,1)S(1)}, u32[]{:S(2)}, u32[]{:S(2)}) collective-permute-start(bf16[4,4,16,768]{3,2,1,0:T(8,128)(2,1)S(1)} %bitcast.590), channel_id=1, source_target_pairs={{0,96},{32,64},{64,32},{96,0},{1,97},{33,65},{65,33},{97,1},{2,98}... | collective-permute-start | bytes 1179656 | tf_op jit(solution)/shard_map/ppermute | solution.py:24
  236.0 15.5 %collective-permute-start.92 = (bf16[4,4,16,768]{3,2,1,0:T(8,128)(2,1)S(1)}, bf16[4,4,16,768]{3,2,1,0:T(8,128)(2,1)S(1)}, u32[]{:S(2)}, u32[]{:S(2)}) collective-permute-start(bf16[4,4,16,768]{3,2,1,0:T(8,128)(2,1)S(1)} %bitcast.589), channel_id=1, source_target_pairs={{0,32},{32,0},{64,96},{96,64},{1,33},{33,1},{65,97},{97,65},{2,34}... | collective-permute-start | bytes 1179656 | tf_op jit(solution)/shard_map/ppermute | solution.py:24
  244.2 12.4 %collective-permute-start.94 = (bf16[4,4,16,768]{3,2,1,0:T(8,128)(2,1)S(1)}, bf16[4,4,16,768]{3,2,1,0:T(8,128)(2,1)S(1)}, u32[]{:S(2)}, u32[]{:S(2)}) collective-permute-start(bf16[4,4,16,768]{3,2,1,0:T(8,128)(2,1)S(1)} %bitcast.588), channel_id=1, source_target_pairs={{0,64},{32,96},{64,0},{96,32},{1,65},{33,97},{65,1},{97,33},{2,66}... | collective-permute-start | bytes 1179656 | tf_op jit(solution)/shard_map/ppermute | solution.py:24
  246.3 33.3 %collective-permute-start.50 = (bf16[4,128,1024]{2,1,0:T(8,128)(2,1)}, bf16[4,128,1024]{2,1,0:T(8,128)(2,1)}, u32[]{:S(2)}, u32[]{:S(2)}) collective-permute-start(bf16[4,128,1024]{2,1,0:T(8,128)(2,1)} %fusion.7), channel_id=1, source_target_pairs={{0,1},{1,0},{2,3},{3,2},{4,5},{5,4},{6,7},{7,6},{8,9},{9,8},{10,11... | collective-permute-start | bytes 3145736 | tf_op jit(solution)/shard_map/ppermute | solution.py:24
  246.4 70.4 %collective-permute-start.42 = (bf16[4,128,1024]{2,1,0:T(8,128)(2,1)}, bf16[4,128,1024]{2,1,0:T(8,128)(2,1)}, u32[]{:S(2)}, u32[]{:S(2)}) collective-permute-start(bf16[4,128,1024]{2,1,0:T(8,128)(2,1)} %fusion.6), channel_id=1, source_target_pairs={{0,1},{1,0},{2,3},{3,2},{4,5},{5,4},{6,7},{7,6},{8,9},{9,8},{10,11... | collective-permute-start | bytes 3145736 | tf_op jit(solution)/shard_map/ppermute | solution.py:24
  256.9 12.9 %collective-permute-start.96 = (bf16[4,16,768]{2,1,0:T(8,128)(2,1)S(1)}, bf16[4,16,768]{2,1,0:T(8,128)(2,1)S(1)}, u32[]{:S(2)}, u32[]{:S(2)}) collective-permute-start(bf16[4,16,768]{2,1,0:T(8,128)(2,1)S(1)} %fusion.71), channel_id=1, source_target_pairs={{0,6},{2,4},{4,2},{6,0},{1,7},{3,5},{5,3},{7,1},{8,14},{10,12},{12... | collective-permute-start | bytes 294920 | tf_op jit(solution)/shard_map/ppermute | solution.py:24
  269.7 16.6 %collective-permute-start.88 = (bf16[24,1024]{1,0:T(8,128)(2,1)}, bf16[24,1024]{1,0:T(8,128)(2,1)}, u32[]{:S(2)}, u32[]{:S(2)}) collective-permute-start(bf16[24,1024]{1,0:T(8,128)(2,1)} %get-tuple-element.142), channel_id=1, source_target_pairs={{0,2},{2,0},{4,6},{6,4},{1,3},{3,1},{5,7},{7,5},{8,10},{10,8},{12,... | collective-permute-start | bytes 147464 | tf_op jit(solution)/shard_map/ppermute | solution.py:24
  271.8 17.3 %collective-permute-start.89 = (bf16[24,1024]{1,0:T(8,128)(2,1)}, bf16[24,1024]{1,0:T(8,128)(2,1)}, u32[]{:S(2)}, u32[]{:S(2)}) collective-permute-start(bf16[24,1024]{1,0:T(8,128)(2,1)} %get-tuple-element.143), channel_id=1, source_target_pairs={{0,6},{2,4},{4,2},{6,0},{1,7},{3,5},{5,3},{7,1},{8,14},{10,12},{12... | collective-permute-start | bytes 147464 | tf_op jit(solution)/shard_map/ppermute | solution.py:24
  273.5 15.6 %collective-permute-start.90 = (bf16[24,1024]{1,0:T(8,128)(2,1)}, bf16[24,1024]{1,0:T(8,128)(2,1)}, u32[]{:S(2)}, u32[]{:S(2)}) collective-permute-start(bf16[24,1024]{1,0:T(8,128)(2,1)} %get-tuple-element.144), channel_id=1, source_target_pairs={{0,4},{2,6},{4,0},{6,2},{1,5},{3,7},{5,1},{7,3},{8,12},{10,14},{12... | collective-permute-start | bytes 147464 | tf_op jit(solution)/shard_map/ppermute | solution.py:24
  275.7 14.9 %all-to-all-start.2 = ((bf16[8,8,768]{2,1,0:T(8,128)(2,1)}), bf16[8,8,768]{2,1,0:T(8,128)(2,1)S(1)}, u32[]{:S(2)}, u32[]{:S(2)}) async-start(bf16[8,8,768]{2,1,0:T(8,128)(2,1)} %bitcast.595), calls=%async_computation.2 | async-start | bytes 196608 | tf_op jit(solution)/shard_map/all_to_all | solution.py:475
  286.4 15.0 %collective-permute-start.53 = (bf16[128,1024]{1,0:T(8,128)(2,1)}, bf16[128,1024]{1,0:T(8,128)(2,1)}, u32[]{:S(2)}, u32[]{:S(2)}) collective-permute-start(bf16[128,1024]{1,0:T(8,128)(2,1)} %get-tuple-element.109), channel_id=1, source_target_pairs={{0,16},{8,24},{16,0},{24,8},{1,17},{9,25},{17,1},{25,9},{2,18},{10... | collective-permute-start | bytes 786440 | tf_op jit(solution)/shard_map/ppermute | solution.py:24
  289.0 14.9 %collective-permute-start.52 = (bf16[128,1024]{1,0:T(8,128)(2,1)}, bf16[128,1024]{1,0:T(8,128)(2,1)}, u32[]{:S(2)}, u32[]{:S(2)}) collective-permute-start(bf16[128,1024]{1,0:T(8,128)(2,1)} %get-tuple-element.110), channel_id=1, source_target_pairs={{0,24},{8,16},{16,8},{24,0},{1,25},{9,17},{17,9},{25,1},{2,26},{10... | collective-permute-start | bytes 786440 | tf_op jit(solution)/shard_map/ppermute | solution.py:24
  307.7 14.6 %collective-permute-start.77 = (bf16[128,1024]{1,0:T(8,128)(2,1)}, bf16[128,1024]{1,0:T(8,128)(2,1)}, u32[]{:S(2)}, u32[]{:S(2)}) collective-permute-start(bf16[128,1024]{1,0:T(8,128)(2,1)} %fusion.97), channel_id=1, source_target_pairs={{0,24},{8,16},{16,8},{24,0},{1,25},{9,17},{17,9},{25,1},{2,26},{10... | collective-permute-start | bytes 786440 | tf_op jit(solution)/shard_map/ppermute | solution.py:24
  308.0 17.1 %collective-permute-start.76 = (bf16[128,1024]{1,0:T(8,128)(2,1)}, bf16[128,1024]{1,0:T(8,128)(2,1)}, u32[]{:S(2)}, u32[]{:S(2)}) collective-permute-start(bf16[128,1024]{1,0:T(8,128)(2,1)} %fusion.97), channel_id=1, source_target_pairs={{0,16},{8,24},{16,0},{24,8},{1,17},{9,25},{17,1},{25,9},{2,18},{10... | collective-permute-start | bytes 786440 | tf_op jit(solution)/shard_map/ppermute | solution.py:24
  308.8 16.4 %collective-permute-start.75 = (bf16[128,1024]{1,0:T(8,128)(2,1)}, bf16[128,1024]{1,0:T(8,128)(2,1)}, u32[]{:S(2)}, u32[]{:S(2)}) collective-permute-start(bf16[128,1024]{1,0:T(8,128)(2,1)} %fusion.97), channel_id=1, source_target_pairs={{0,8},{8,0},{16,24},{24,16},{1,9},{9,1},{17,25},{25,17},{2,10},{10... | collective-permute-start | bytes 786440 | tf_op jit(solution)/shard_map/ppermute | solution.py:24
  328.0 89.6 %collective-permute-start.78 = (bf16[4,128,1024]{2,1,0:T(8,128)(2,1)}, bf16[4,128,1024]{2,1,0:T(8,128)(2,1)}, u32[]{:S(2)}, u32[]{:S(2)}) collective-permute-start(bf16[4,128,1024]{2,1,0:T(8,128)(2,1)} %get-tuple-element.104), channel_id=1, source_target_pairs={{0,1},{1,0},{2,3},{3,2},{4,5},{5,4},{6,7},{7,6},{8,9},{9,8},{10,11... | collective-permute-start | bytes 3145736 | tf_op jit(solution)/shard_map/ppermute | solution.py:24
  375.1 40.0 %collective-permute-start.60 = (bf16[1024,256]{1,0:T(8,128)(2,1)S(1)}, bf16[1024,256]{1,0:T(8,128)(2,1)S(1)}, u32[]{:S(2)}, u32[]{:S(2)}) collective-permute-start(bf16[1024,256]{1,0:T(8,128)(2,1)S(1)} %get-tuple-element.59), channel_id=1, source_target_pairs={{0,6},{2,4},{4,2},{6,0},{1,7},{3,5},{5,3},{7,1},{8,14},{10,12},{12... | collective-permute-start | bytes 1572872 | tf_op jit(solution)/shard_map/ppermute | solution.py:24
  377.7 37.4 %collective-permute-start.58 = (bf16[1024,256]{1,0:T(8,128)(2,1)S(1)}, bf16[1024,256]{1,0:T(8,128)(2,1)S(1)}, u32[]{:S(2)}, u32[]{:S(2)}) collective-permute-start(bf16[1024,256]{1,0:T(8,128)(2,1)S(1)} %get-tuple-element.57), channel_id=1, source_target_pairs={{0,2},{2,0},{4,6},{6,4},{1,3},{3,1},{5,7},{7,5},{8,10},{10,8},{12,... | collective-permute-start | bytes 1572872 | tf_op jit(solution)/shard_map/ppermute | solution.py:24
  377.7 39.5 %collective-permute-start.59 = (bf16[1024,256]{1,0:T(8,128)(2,1)S(1)}, bf16[1024,256]{1,0:T(8,128)(2,1)S(1)}, u32[]{:S(2)}, u32[]{:S(2)}) collective-permute-start(bf16[1024,256]{1,0:T(8,128)(2,1)S(1)} %get-tuple-element.58), channel_id=1, source_target_pairs={{0,4},{2,6},{4,0},{6,2},{1,5},{3,7},{5,1},{7,3},{8,12},{10,14},{12... | collective-permute-start | bytes 1572872 | tf_op jit(solution)/shard_map/ppermute | solution.py:24
  412.4 15.2 %collective-permute-start.64 = (bf16[1024,256]{1,0:T(8,128)(2,1)S(1)}, bf16[1024,256]{1,0:T(8,128)(2,1)S(1)}, u32[]{:S(2)}, u32[]{:S(2)}) collective-permute-start(bf16[1024,256]{1,0:T(8,128)(2,1)S(1)} %get-tuple-element.62), channel_id=1, source_target_pairs={{0,6},{2,4},{4,2},{6,0},{1,7},{3,5},{5,3},{7,1},{8,14},{10,12},{12... | collective-permute-start | bytes 1572872 | tf_op jit(solution)/shard_map/ppermute | solution.py:24
  415.1 14.9 %collective-permute-start.62 = (bf16[1024,256]{1,0:T(8,128)(2,1)S(1)}, bf16[1024,256]{1,0:T(8,128)(2,1)S(1)}, u32[]{:S(2)}, u32[]{:S(2)}) collective-permute-start(bf16[1024,256]{1,0:T(8,128)(2,1)S(1)} %get-tuple-element.60), channel_id=1, source_target_pairs={{0,2},{2,0},{4,6},{6,4},{1,3},{3,1},{5,7},{7,5},{8,10},{10,8},{12,... | collective-permute-start | bytes 1572872 | tf_op jit(solution)/shard_map/ppermute | solution.py:24
  415.1 23.8 %collective-permute-start.63 = (bf16[1024,256]{1,0:T(8,128)(2,1)S(1)}, bf16[1024,256]{1,0:T(8,128)(2,1)S(1)}, u32[]{:S(2)}, u32[]{:S(2)}) collective-permute-start(bf16[1024,256]{1,0:T(8,128)(2,1)S(1)} %get-tuple-element.61), channel_id=1, source_target_pairs={{0,4},{2,6},{4,0},{6,2},{1,5},{3,7},{5,1},{7,3},{8,12},{10,14},{12... | collective-permute-start | bytes 1572872 | tf_op jit(solution)/shard_map/ppermute | solution.py:24
  417.5 21.3 %collective-permute-start.61 = (bf16[1024,256]{1,0:T(8,128)(2,1)S(1)}, bf16[1024,256]{1,0:T(8,128)(2,1)S(1)}, u32[]{:S(2)}, u32[]{:S(2)}) collective-permute-start(bf16[1024,256]{1,0:T(8,128)(2,1)S(1)} %add_convert_fusion.1), channel_id=1, source_target_pairs={{0,32},{32,0},{1,33},{33,1},{2,34},{34,2},{3,35},{35,3},{4,36},{36... | collective-permute-start | bytes 1572872 | tf_op jit(solution)/shard_map/ppermute | solution.py:24
  420.0 23.2 %collective-permute-start.80 = (bf16[4,16,1024]{2,1,0:T(8,128)(2,1)S(1)}, bf16[4,16,1024]{2,1,0:T(8,128)(2,1)S(1)}, u32[]{:S(2)}, u32[]{:S(2)}) collective-permute-start(bf16[4,16,1024]{2,1,0:T(8,128)(2,1)S(1)} %bitcast.618), channel_id=1, source_target_pairs={{0,96},{32,64},{64,32},{96,0},{1,97},{33,65},{65,33},{97,1},{2,98}... | collective-permute-start | bytes 393224 | tf_op jit(solution)/shard_map/ppermute | solution.py:24
  427.7 15.5 %collective-permute-start.79 = (bf16[4,16,1024]{2,1,0:T(8,128)(2,1)S(1)}, bf16[4,16,1024]{2,1,0:T(8,128)(2,1)S(1)}, u32[]{:S(2)}, u32[]{:S(2)}) collective-permute-start(bf16[4,16,1024]{2,1,0:T(8,128)(2,1)S(1)} %bitcast.617), channel_id=1, source_target_pairs={{0,32},{32,0},{64,96},{96,64},{1,33},{33,1},{65,97},{97,65},{2,34}... | collective-permute-start | bytes 393224 | tf_op jit(solution)/shard_map/ppermute | solution.py:24
  429.9 13.3 %collective-permute-start.81 = (bf16[4,16,1024]{2,1,0:T(8,128)(2,1)S(1)}, bf16[4,16,1024]{2,1,0:T(8,128)(2,1)S(1)}, u32[]{:S(2)}, u32[]{:S(2)}) collective-permute-start(bf16[4,16,1024]{2,1,0:T(8,128)(2,1)S(1)} %bitcast.616), channel_id=1, source_target_pairs={{0,64},{32,96},{64,0},{96,32},{1,65},{33,97},{65,1},{97,33},{2,66}... | collective-permute-start | bytes 393224 | tf_op jit(solution)/shard_map/ppermute | solution.py:24
  449.2 18.8 %collective-permute-start.65 = (bf16[4,128,1024]{2,1,0:T(8,128)(2,1)S(1)}, bf16[4,128,1024]{2,1,0:T(8,128)(2,1)S(1)}, u32[]{:S(2)}, u32[]{:S(2)}) collective-permute-start(bf16[4,128,1024]{2,1,0:T(8,128)(2,1)S(1)} %fusion.8), channel_id=1, source_target_pairs={{0,1},{1,0},{2,3},{3,2},{4,5},{5,4},{6,7},{7,6},{8,9},{9,8},{10,11... | collective-permute-start | bytes 3145736 | tf_op jit(solution)/shard_map/ppermute | solution.py:24
  452.5 15.3 %collective-permute-start.71 = (bf16[4,4,16,512]{3,2,1,0:T(8,128)(2,1)S(1)}, bf16[4,4,16,512]{3,2,1,0:T(8,128)(2,1)S(1)}, u32[]{:S(2)}, u32[]{:S(2)}) collective-permute-start(bf16[4,4,16,512]{3,2,1,0:T(8,128)(2,1)S(1)} %bitcast.598), channel_id=1, source_target_pairs={{0,64},{32,96},{64,0},{96,32},{1,65},{33,97},{65,1},{97,33},{2,66}... | collective-permute-start | bytes 786440 | tf_op jit(solution)/shard_map/ppermute | solution.py:24
  454.4 47.2 %collective-permute-start.91 = (bf16[40,1024]{1,0:T(8,128)(2,1)S(1)}, bf16[40,1024]{1,0:T(8,128)(2,1)S(1)}, u32[]{:S(2)}, u32[]{:S(2)}) collective-permute-start(bf16[40,1024]{1,0:T(8,128)(2,1)S(1)} %pad_maximum_fusion.26), channel_id=1, source_target_pairs={{0,0},{2,1},{4,2},{6,3},{32,4},{34,5},{36,6},{38,7},{64,8},{66,9},... | collective-permute-start | bytes 245768 | tf_op jit(solution)/shard_map/ppermute | solution.py:484
  470.9 13.1 %collective-permute-start.68 = (bf16[128,1024]{1,0:T(8,128)(2,1)S(1)}, bf16[128,1024]{1,0:T(8,128)(2,1)S(1)}, u32[]{:S(2)}, u32[]{:S(2)}) collective-permute-start(bf16[128,1024]{1,0:T(8,128)(2,1)S(1)} %get-tuple-element.106), channel_id=1, source_target_pairs={{0,16},{8,24},{16,0},{24,8},{1,17},{9,25},{17,1},{25,9},{2,18},{10... | collective-permute-start | bytes 786440 | tf_op jit(solution)/shard_map/ppermute | solution.py:24
  473.4 13.2 %collective-permute-start.67 = (bf16[128,1024]{1,0:T(8,128)(2,1)S(1)}, bf16[128,1024]{1,0:T(8,128)(2,1)S(1)}, u32[]{:S(2)}, u32[]{:S(2)}) collective-permute-start(bf16[128,1024]{1,0:T(8,128)(2,1)S(1)} %get-tuple-element.107), channel_id=1, source_target_pairs={{0,24},{8,16},{16,8},{24,0},{1,25},{9,17},{17,9},{25,1},{2,26},{10... | collective-permute-start | bytes 786440 | tf_op jit(solution)/shard_map/ppermute | solution.py:24
  473.6 14.7 %collective-permute-start.73 = (bf16[4,16,512]{2,1,0:T(8,128)(2,1)S(1)}, bf16[4,16,512]{2,1,0:T(8,128)(2,1)S(1)}, u32[]{:S(2)}, u32[]{:S(2)}) collective-permute-start(bf16[4,16,512]{2,1,0:T(8,128)(2,1)S(1)} %fusion.77), channel_id=1, source_target_pairs={{0,6},{2,4},{4,2},{6,0},{1,7},{3,5},{5,3},{7,1},{8,14},{10,12},{12... | collective-permute-start | bytes 196616 | tf_op jit(solution)/shard_map/ppermute | solution.py:24
  490.5 15.1 %all-to-all-start.1 = ((bf16[8,8,512]{2,1,0:T(8,128)(2,1)}), bf16[8,8,512]{2,1,0:T(8,128)(2,1)S(1)}, u32[]{:S(2)}, u32[]{:S(2)}) async-start(bf16[8,8,512]{2,1,0:T(8,128)(2,1)} %bitcast.146), calls=%async_computation.1 | async-start | bytes 131072 | tf_op jit(solution)/shard_map/all_to_all | solution.py:475
  499.7 18.2 %collective-permute-start.43 = (bf16[128,1024]{1,0:T(8,128)(2,1)}, bf16[128,1024]{1,0:T(8,128)(2,1)S(1)}, u32[]{:S(2)}, u32[]{:S(2)}) collective-permute-start(bf16[128,1024]{1,0:T(8,128)(2,1)} %get-tuple-element.113), channel_id=1, source_target_pairs={{0,8},{8,0},{16,24},{24,16},{1,9},{9,1},{17,25},{25,17},{2,10},{10... | collective-permute-start | bytes 786440 | tf_op jit(solution)/shard_map/ppermute | solution.py:24
  501.6 17.0 %collective-permute-start.45 = (bf16[128,1024]{1,0:T(8,128)(2,1)}, bf16[128,1024]{1,0:T(8,128)(2,1)S(1)}, u32[]{:S(2)}, u32[]{:S(2)}) collective-permute-start(bf16[128,1024]{1,0:T(8,128)(2,1)} %get-tuple-element.114), channel_id=1, source_target_pairs={{0,16},{8,24},{16,0},{24,8},{1,17},{9,25},{17,1},{25,9},{2,18},{10... | collective-permute-start | bytes 786440 | tf_op jit(solution)/shard_map/ppermute | solution.py:24
  505.6 14.0 %collective-permute-start.44 = (bf16[128,1024]{1,0:T(8,128)(2,1)}, bf16[128,1024]{1,0:T(8,128)(2,1)S(1)}, u32[]{:S(2)}, u32[]{:S(2)}) collective-permute-start(bf16[128,1024]{1,0:T(8,128)(2,1)} %get-tuple-element.115), channel_id=1, source_target_pairs={{0,24},{8,16},{16,8},{24,0},{1,25},{9,17},{17,9},{25,1},{2,26},{10... | collective-permute-start | bytes 786440 | tf_op jit(solution)/shard_map/ppermute | solution.py:24
  (102 other events, 1315.8 us)
